TPU v7x, 32 devices: a whole 2x2x4 slice. The times are simulated.
32 devices in a mesh: dp: 16 (over z, y, x), narrow: 2 (over core).
Axes of the slice: x: 2, y: 2, z: 4, core: 2. Of those that a mesh axis runs over, the one named last changes fastest.
Arguments:
- tokens: bfloat16 [16384, 768], P(('dp', 'narrow')), may hold values from -6 to 6
- cotangent: bfloat16 [16384, 768], P(('dp', 'narrow')), may hold values from -6 to 6
- gains: float32 [2, 768], replicated, may hold values from 0.5 to 1.5
- gain_moments: float32 [2, 768], replicated, may hold values from 10485 to 41943
- qkv_master: float32 [3, 2, 128, 48, 48], P(None, 'narrow', 'dp'), may hold values from -0.21875 to 0.21875
- out_master: float32 [2, 128, 48, 48], P('narrow', 'dp'), may hold values from -1.25 to 1.25
- ffn_master: float32 [2, 2, 128, 48, 128], P(None, 'narrow', 'dp'), may hold values from -0.21875 to 0.21875
- down_master: float32 [2, 128, 128, 48], P('narrow', 'dp'), may hold values from -0.125 to 0.125
- attn_left: float32 [4, 2, 128, 48, 48], P(None, 'narrow', 'dp'), as said below
- attn_right: float32 [4, 2, 128, 48, 48], P(None, 'narrow', 'dp'), as said below
- attn_left_root: float32 [4, 2, 128, 48, 48], P(None, 'narrow', 'dp'), as said below
- attn_right_root: float32 [4, 2, 128, 48, 48], P(None, 'narrow', 'dp'), as said below
- ffn_left: float32 [2, 2, 128, 48, 48], P(None, 'narrow', 'dp'), as said below
- ffn_right: float32 [2, 2, 128, 128, 128], P(None, 'narrow', 'dp'), as said below
- ffn_left_root: float32 [2, 2, 128, 48, 48], P(None, 'narrow', 'dp'), as said below
- ffn_right_root: float32 [2, 2, 128, 128, 128], P(None, 'narrow', 'dp'), as said below
- down_left: float32 [2, 128, 128, 128], P('narrow', 'dp'), as said below
- down_right: float32 [2, 128, 48, 48], P('narrow', 'dp'), as said below
- down_left_root: float32 [2, 128, 128, 128], P('narrow', 'dp'), as said below
- down_right_root: float32 [2, 128, 48, 48], P('narrow', 'dp'), as said below
Outputs:
- layer_out: bfloat16 [16384, 768], P(('dp', 'narrow'))
- input_grad: float32 [16384, 768], P(('dp', 'narrow'))
- gain_grad: float32 [2, 768], replicated
- gain_moment_new: float32 [2, 768], replicated
- gain_new: float32 [2, 768], replicated
- attn_grad: float32 [4, 2, 128, 48, 48], P(None, 'narrow', 'dp')
- attn_left_new: float32 [4, 2, 128, 48, 48], P(None, 'narrow', 'dp')
- attn_right_new: float32 [4, 2, 128, 48, 48], P(None, 'narrow', 'dp')
- qkv_new: float32 [3, 2, 128, 48, 48], P(None, 'narrow', 'dp')
- out_new: float32 [2, 128, 48, 48], P('narrow', 'dp')
- ffn_grad: float32 [2, 2, 128, 48, 128], P(None, 'narrow', 'dp')
- ffn_left_new: float32 [2, 2, 128, 48, 48], P(None, 'narrow', 'dp')
- ffn_right_new: float32 [2, 2, 128, 128, 128], P(None, 'narrow', 'dp')
- ffn_new: float32 [2, 2, 128, 48, 128], P(None, 'narrow', 'dp')
- down_grad: float32 [2, 128, 128, 48], P('narrow', 'dp')
- down_left_new: float32 [2, 128, 128, 128], P('narrow', 'dp')
- down_right_new: float32 [2, 128, 48, 48], P('narrow', 'dp')
- down_new: float32 [2, 128, 128, 48], P('narrow', 'dp')
Inputs may be any that keep to these rules, and one draw needn't show every extreme that they name: `attn_left`: symmetric positive definite blocks. `attn_right`: symmetric positive definite blocks. `attn_left_root`: symmetric blocks. `attn_right_root`: symmetric blocks. `ffn_left`: symmetric positive definite blocks. `ffn_right`: symmetric positive definite blocks. `ffn_left_root`: symmetric blocks. `ffn_right_root`: symmetric blocks. `down_left`: symmetric positive definite blocks. `down_right`: symmetric positive definite blocks. `down_left_root`: symmetric blocks. `down_right_root`: symmetric blocks.
All inputs are finite; a program needn't handle non-finite values.
Results may differ from a plain program's by a relative error of at most 0.014.
Values may be sent and summed in bfloat16 or wider, within the bound.
No kernel may reach another device: no remote copies, remote signals or barrier semaphores. Data moves between devices by JAX's collectives and lax.ppermute only.
A program may use at most 192 MiB of HBM per device.

v0:
```python
import functools
import math

import jax
import jax.numpy as jnp
from jax import lax
from jax.experimental import pallas as pl
from jax.experimental.pallas import tpu as pltpu
from jax.sharding import PartitionSpec as P

D = 768
HEAD_DIM = 64
FF = 2048
LEN = 1024
GRID = 16
DBLK = D // GRID
FBLK = FF // GRID
HALF_GRID = GRID // 2
HALF_D = D // 2
HALF_FF = FF // 2
PAIR = 2 * HEAD_DIM
ROWS = 256

EPSILON = 1e-05
DECAY = 0.5
STEP_RATE = 0.25
GAIN_RATE = 0.1
NEG_FILL = -1e30
HIGHEST_PRECISION = lax.Precision.HIGHEST
BF16 = jnp.bfloat16
F32 = jnp.float32
VMEM_MIB = 18
DENSE_ROWS = 512
TILE = 256
WIDE_TILE = 512
SMALL_MIB = 8
PACK_MIB = 60
STATE_ROWS = 16


def dot_nn(left, right):
    return lax.dot_general(left, right, (((1,), (0,)), ((), ())), preferred_element_type=F32)


def dot_nt(left, right):
    return lax.dot_general(left, right, (((1,), (1,)), ((), ())), preferred_element_type=F32)


def dot_tn(left, right):
    return lax.dot_general(left, right, (((0,), (0,)), ((), ())), preferred_element_type=F32)


def kernel_params(mib=VMEM_MIB):
    return pltpu.CompilerParams(vmem_limit_bytes=mib * 1024 * 1024)


def cost():
    return pl.CostEstimate(flops=0, bytes_accessed=0, transcendentals=0)


def whole_call(kernel, inputs, shapes, name, scalars=0, mib=SMALL_MIB, scratch=()):
    vmem = pl.BlockSpec(memory_space=pltpu.VMEM)
    smem = pl.BlockSpec(memory_space=pltpu.SMEM)
    return pl.pallas_call(
        kernel,
        in_specs=[smem] * scalars + [vmem] * (len(inputs) - scalars),
        out_specs=[vmem] * len(shapes),
        out_shape=shapes,
        scratch_shapes=list(scratch),
        compiler_params=kernel_params(mib),
        cost_estimate=cost(),
        name=name,
    )(*inputs)


def over_rows(length, rows, work):
    @pl.loop(0, length // rows)
    def _(step):
        work(pl.ds(pl.multiple_of(step * rows, rows), rows))


def lower_lanes(shape):
    return lax.broadcasted_iota(jnp.int32, shape, 1) % HEAD_DIM < HEAD_DIM // 2


def turn(features, cosine, sine_part, lower):
    half = HEAD_DIM // 2
    partner = jnp.where(
        lower, pltpu.roll(features, PAIR - half, 1), pltpu.roll(features, half, 1)
    )
    return features * cosine + partner * sine_part


def project_kernel(x_ref, gain_ref, w_ref, cos_ref, sin_ref, n1_ref, q_ref, k_ref, v_ref):
    lower = lower_lanes((DENSE_ROWS, PAIR))

    def work(rows):
        x = x_ref[rows, :].astype(F32)
        scale = lax.rsqrt(jnp.mean(x * x, -1, keepdims=True) + EPSILON)
        normed = (x * scale * gain_ref[0:1, :]).astype(BF16)
        n1_ref[rows, :] = normed
        cosine, sine_part = cos_ref[rows, :], sin_ref[rows, :]
        both = dot_nn(normed, w_ref[...])
        for tile in range(HALF_D // PAIR):
            lanes = slice(tile * PAIR, (tile + 1) * PAIR)
            query = both[:, tile * PAIR : (tile + 1) * PAIR]
            key = both[:, HALF_D + tile * PAIR : HALF_D + (tile + 1) * PAIR]
            turned = turn(query, cosine, sine_part, lower).astype(BF16)
            q_ref[rows, lanes] = turned * BF16(1.0 / math.sqrt(HEAD_DIM))
            k_ref[rows, lanes] = turn(key, cosine, sine_part, lower).astype(BF16)
        v_ref[rows, :] = both[:, 2 * HALF_D :].astype(BF16)

    over_rows(x_ref.shape[0], DENSE_ROWS, work)


def project(x, gains, weight, cosine, sine_part):
    length = x.shape[0]
    half = jax.ShapeDtypeStruct((length, HALF_D), BF16)
    shapes = [jax.ShapeDtypeStruct((length, D), BF16), half, half, half]
    return whole_call(
        project_kernel, [x, gains, weight, cosine, sine_part], shapes, "project", mib=VMEM_MIB
    )


def attend_kernel(q_ref, k_ref, v_ref, o_ref, lse_ref):
    @pl.loop(0, q_ref.shape[1] // PAIR)
    def _(pair):
        lanes = pl.ds(pl.multiple_of(pair * PAIR, PAIR), PAIR)
        rows = pl.ds(pl.multiple_of(pair * 8, 8), 8)
        attend_pair(
            *(ref.at[:, lanes] for ref in (q_ref, k_ref, v_ref, o_ref)), lse_ref.at[rows, :]
        )


def attend_pair(q_ref, k_ref, v_ref, o_ref, lse_ref):
    length = q_ref.shape[0]
    first_head = lax.broadcasted_iota(jnp.int32, (ROWS, PAIR), 1) < HEAD_DIM
    keys = k_ref[...]
    values = jnp.concatenate([v_ref[...], jnp.ones((length, PAIR), BF16)], 1)
    causal = lax.broadcasted_iota(jnp.int32, (2 * ROWS, ROWS), 0) % ROWS >= (
        lax.broadcasted_iota(jnp.int32, (2 * ROWS, ROWS), 1)
    )
    for block in range(length // ROWS):
        rows = slice(block * ROWS, (block + 1) * ROWS)
        width = (block + 1) * ROWS
        query_block = q_ref[rows, :]
        zero = jnp.zeros_like(query_block)
        query = jnp.concatenate(
            [jnp.where(first_head, query_block, zero), jnp.where(first_head, zero, query_block)], 0
        )
        scores = jnp.where(causal, dot_nt(query, keys[block * ROWS : width]), NEG_FILL)
        if block:
            scores = jnp.concatenate([dot_nt(query, keys[: block * ROWS]), scores], 1)
        top = jnp.max(scores, 1, keepdims=True)
        exponent = jnp.exp(scores - top).astype(BF16)
        product = dot_nn(exponent, values[:width])
        total = product[:, PAIR:]
        out = product[:, :PAIR] / total
        sums = top + jnp.log(total)
        o_ref[rows, :] = jnp.where(first_head, out[:ROWS], out[ROWS:]).astype(BF16)
        lane = lax.broadcasted_iota(jnp.int32, (ROWS, PAIR), 1)
        lse_ref[:, rows] = jnp.transpose(jnp.where(lane == 0, sums[:ROWS], sums[ROWS:]))[:8, :]


def attend(q, k, v):
    length = q.shape[0]
    shapes = [
        jax.ShapeDtypeStruct(q.shape, BF16),
        jax.ShapeDtypeStruct((8 * (q.shape[1] // PAIR), length), F32),
    ]
    return whole_call(attend_kernel, [q, k, v], shapes, "attend", mib=VMEM_MIB)


def attend_back_kernel(
    q_ref, k_ref, v_ref, do_ref, o_ref, lse_ref, cos_ref, sin_ref, grad_ref, dqt_ref
):
    @pl.loop(0, q_ref.shape[1] // PAIR)
    def _(pair):
        lanes = pl.ds(pl.multiple_of(pair * PAIR, PAIR), PAIR)
        rows = pl.ds(pl.multiple_of(pair * 8, 8), 8)
        attend_back_pair(
            *(ref.at[:, lanes] for ref in (q_ref, k_ref, v_ref, do_ref, o_ref)),
            lse_ref.at[rows, :],
            cos_ref,
            sin_ref,
            *(
                grad_ref.at[:, pl.ds(pl.multiple_of(at * HALF_D + pair * PAIR, PAIR), PAIR)]
                for at in range(3)
            ),
            dqt_ref,
        )


def attend_back_pair(
    q_ref, k_ref, v_ref, do_ref, o_ref, lse_ref, cos_ref, sin_ref, dq_ref, dk_ref, dv_ref, dqt_ref
):
    length = q_ref.shape[0]
    first_head = lax.broadcasted_iota(jnp.int32, (length, PAIR), 1) < HEAD_DIM
    zero = BF16(0)
    queries = [
        jnp.where(first_head, q_ref[...], zero),
        jnp.where(first_head, zero, q_ref[...]),
    ]
    grads = [
        jnp.where(first_head, do_ref[...], zero),
        jnp.where(first_head, zero, do_ref[...]),
    ]
    product = do_ref[...].astype(F32) * o_ref[...].astype(F32)
    head_row = lax.broadcasted_iota(jnp.int32, (8, PAIR), 0)
    head_lane = lax.broadcasted_iota(jnp.int32, (8, PAIR), 1) // HEAD_DIM
    inner = lax.dot_general(
        (head_row == head_lane).astype(F32),
        product,
        (((1,), (1,)), ((), ())),
        preferred_element_type=F32,
        precision=HIGHEST_PRECISION,
    )
    turned_keys = jnp.transpose(k_ref[...].astype(F32)).astype(BF16)
    first_rows = lax.broadcasted_iota(jnp.int32, turned_keys.shape, 0) < HEAD_DIM
    key_heads = [
        jnp.where(first_rows, turned_keys, zero),
        jnp.where(first_rows, zero, turned_keys),
    ]
    causal = lax.broadcasted_iota(jnp.int32, (ROWS, ROWS), 0) <= lax.broadcasted_iota(
        jnp.int32, (ROWS, ROWS), 1
    )
    dqt_ref[...] = jnp.zeros_like(dqt_ref)
    lower = lower_lanes((ROWS, PAIR))
    for block in range(length // ROWS):
        rows = slice(block * ROWS, (block + 1) * ROWS)
        start = block * ROWS
        key_block, value_block = k_ref[rows, :], v_ref[rows, :]
        dk = jnp.zeros((ROWS, PAIR), F32)
        dv = jnp.zeros((ROWS, PAIR), F32)
        for head in range(2):
            scores = dot_nt(key_block, queries[head][start:])
            probs = jnp.exp(scores - lse_ref[head : head + 1, start:])
            diagonal = jnp.where(causal, probs[:, :ROWS], 0.0)
            if start + ROWS == length:
                probs = diagonal
            else:
                probs = jnp.concatenate([diagonal, probs[:, ROWS:]], 1)
            prob_grad = dot_nt(value_block, grads[head][start:])
            score_grad = (probs * (prob_grad - inner[head : head + 1, start:])).astype(BF16)
            dv = dv + dot_nn(probs.astype(BF16), grads[head][start:])
            dk = dk + dot_nn(score_grad, queries[head][start:])
            dqt_ref[:, start:] += dot_nn(key_heads[head][:, rows], score_grad)
        dk_ref[rows, :] = turn(dk, cos_ref[rows, :], -sin_ref[rows, :], lower).astype(BF16)
        dv_ref[rows, :] = dv.astype(BF16)
    for block in range(length // ROWS):
        rows = slice(block * ROWS, (block + 1) * ROWS)
        dq = jnp.transpose(dqt_ref[:, rows]) * (1.0 / math.sqrt(HEAD_DIM))
        dq_ref[rows, :] = turn(dq, cos_ref[rows, :], -sin_ref[rows, :], lower).astype(BF16)


def attend_back(q, k, v, grad, o, lse, cosine, sine_part):
    return whole_call(
        attend_back_kernel,
        [q, k, v, grad, o, lse, cosine, sine_part],
        [jax.ShapeDtypeStruct((q.shape[0], 3 * q.shape[1]), BF16)],
        "attend_back",
        mib=VMEM_MIB,
        scratch=[pltpu.VMEM((PAIR, q.shape[0]), F32)],
    )[0]


def ffn_kernel(
    x_ref, o_ref, o_far_ref, wo_ref, wo_far_ref, gain_ref, wg_ref, wu_ref,
    x1_ref, n2_ref, gate_ref, up_ref, hidden_ref,
):
    def work(rows):
        middle = (
            x_ref[rows, :].astype(F32)
            + dot_nn(o_ref[rows, :], wo_ref[...])
            + dot_nn(o_far_ref[rows, :], wo_far_ref[...])
        )
        x1_ref[rows, :] = middle
        scale = lax.rsqrt(jnp.mean(middle * middle, -1, keepdims=True) + EPSILON)
        normed = (middle * scale * gain_ref[1:2, :]).astype(BF16)
        n2_ref[rows, :] = normed

        @pl.loop(0, HALF_FF // TILE)
        def _(tile):
            lanes = pl.ds(pl.multiple_of(tile * TILE, TILE), TILE)
            gate = dot_nn(n2_ref[rows, :], wg_ref[:, lanes])
            up = dot_nn(n2_ref[rows, :], wu_ref[:, lanes])
            gate_ref[rows, lanes] = gate
            up_ref[rows, lanes] = up
            hidden_ref[rows, lanes] = (gate * jax.nn.sigmoid(gate) * up).astype(BF16)

    over_rows(x_ref.shape[0], DENSE_ROWS, work)


def ffn(*inputs):
    length = inputs[0].shape[0]
    shapes = [
        jax.ShapeDtypeStruct((length, width), kind)
        for width, kind in ((D, F32), (D, BF16), (HALF_FF, F32), (HALF_FF, F32), (HALF_FF, BF16))
    ]
    return whole_call(ffn_kernel, inputs, shapes, "ffn", mib=VMEM_MIB)


def ffn_out_kernel(hidden_ref, wdt_ref, part_ref):
    def work(rows):
        part_ref[rows, :] = dot_nt(hidden_ref[rows, :], wdt_ref[...]).astype(BF16)

    over_rows(hidden_ref.shape[0], DENSE_ROWS, work)


def ffn_out(hidden, wdt):
    shape = jax.ShapeDtypeStruct((hidden.shape[0], D), BF16)
    return whole_call(ffn_out_kernel, [hidden, wdt], [shape], "ffn_out", mib=VMEM_MIB)[0]


def ffn_back_kernel(cot_ref, gate_ref, up_ref, wdt_ref, wg_ref, wu_ref, dgu_ref, dn2_ref):
    def work(rows):
        @pl.loop(0, HALF_FF // WIDE_TILE)
        def _(tile):
            lanes = pl.ds(pl.multiple_of(tile * WIDE_TILE, WIDE_TILE), WIDE_TILE)
            up_lanes = pl.ds(pl.multiple_of(HALF_FF + tile * WIDE_TILE, WIDE_TILE), WIDE_TILE)
            hidden_grad = dot_nn(cot_ref[rows, :], wdt_ref[:, lanes])
            gate, up = gate_ref[rows, lanes], up_ref[rows, lanes]
            sigma = jax.nn.sigmoid(gate)
            gate_grad = hidden_grad * up * sigma * (1.0 + gate * (1.0 - sigma))
            dgu_ref[rows, lanes] = gate_grad.astype(BF16)
            dgu_ref[rows, up_lanes] = (hidden_grad * gate * sigma).astype(BF16)

        @pl.loop(0, D // TILE)
        def _(tile):
            lanes = pl.ds(pl.multiple_of(tile * TILE, TILE), TILE)
            dn2 = dot_nt(dgu_ref[rows, :HALF_FF], wg_ref[lanes, :]) + dot_nt(
                dgu_ref[rows, HALF_FF:], wu_ref[lanes, :]
            )
            dn2_ref[rows, lanes] = dn2.astype(BF16)

    over_rows(cot_ref.shape[0], DENSE_ROWS, work)


def ffn_back(cot, gate, up, wdt, wg, wu):
    shapes = [jax.ShapeDtypeStruct((cot.shape[0], width), BF16) for width in (FF, D)]
    return whole_call(
        ffn_back_kernel, [cot, gate, up, wdt, wg, wu], shapes, "ffn_back", mib=VMEM_MIB
    )


def middle_back_kernel(
    cot_ref, x1_ref, near_ref, far_ref, gain_ref, wo_ref, dx1_ref, da_ref, do_ref, g2_ref
):
    g2_ref[...] = jnp.zeros_like(g2_ref)

    def work(rows):
        middle = x1_ref[rows, :]
        scale = lax.rsqrt(jnp.mean(middle * middle, -1, keepdims=True) + EPSILON)
        grad = near_ref[rows, :].astype(F32) + far_ref[rows, :].astype(F32)
        weighted = grad * gain_ref[1:2, :]
        inner = jnp.mean(weighted * middle, -1, keepdims=True)
        middle_grad = (
            cot_ref[rows, :].astype(F32)
            + scale * weighted
            - middle * (scale * scale * scale * inner)
        )
        dx1_ref[rows, :] = middle_grad
        branch = middle_grad.astype(BF16)
        da_ref[rows, :] = branch
        do_ref[rows, :] = dot_nt(branch, wo_ref[...]).astype(BF16)
        g2_ref[...] += jnp.sum(grad * middle * scale, 0, keepdims=True)

    over_rows(cot_ref.shape[0], DENSE_ROWS, work)


def middle_back(*inputs):
    length = inputs[0].shape[0]
    shapes = [
        jax.ShapeDtypeStruct(shape, kind)
        for shape, kind in (
            ((length, D), F32),
            ((length, D), BF16),
            ((length, HALF_D), BF16),
            ((1, D), F32),
        )
    ]
    return whole_call(middle_back_kernel, inputs, shapes, "middle_back", mib=VMEM_MIB)


def input_back_kernel(x_ref, dqkv_ref, w_ref, part_ref, g1_ref):
    g1_ref[...] = jnp.zeros_like(g1_ref)

    def work(rows):
        grad = dot_nt(dqkv_ref[rows, :], w_ref[...])
        part_ref[rows, :] = grad.astype(BF16)
        x = x_ref[rows, :].astype(F32)
        scale = lax.rsqrt(jnp.mean(x * x, -1, keepdims=True) + EPSILON)
        g1_ref[...] += jnp.sum(grad * x * scale, 0, keepdims=True)

    over_rows(x_ref.shape[0], DENSE_ROWS, work)


def input_back(x, dqkv, w):
    shapes = [jax.ShapeDtypeStruct(x.shape, BF16), jax.ShapeDtypeStruct((1, D), F32)]
    return whole_call(input_back_kernel, [x, dqkv, w], shapes, "input_back", mib=VMEM_MIB)


def pair_up(bit, count):
    return [(i, i ^ bit) for i in range(count)]


def after(value, *others):
    return lax.optimization_barrier((value,) + others)[0]


def along(values, bit, count):
    return lax.ppermute(values, "dp", pair_up(bit, count))


def shifted(values, steps, count):
    return lax.ppermute(values, "dp", [(i, (i + 4 * steps) % count) for i in range(count)])


def other_core(values):
    return lax.ppermute(values, "narrow", [(0, 1), (1, 0)])


def all_shifted(values, count):
    return [shifted(values, step, count) for step in range(1, count // 4)]


def copy_columns(sources, outputs, name):
    rows = sources[0].shape[0]
    shapes = [
        jax.ShapeDtypeStruct((rows, sum(stop - start for _, start, stop in parts)), BF16)
        for parts in outputs
    ]

    def kernel(*refs):
        for out_ref, parts in zip(refs[len(sources) :], outputs):
            at = 0
            for number, start, stop in parts:
                out_ref[:, at : at + stop - start] = refs[number][:, start:stop]
                at += stop - start

    return whole_call(kernel, sources, shapes, name)


def block_rows(owner):
    return pl.ds(pl.multiple_of(owner * DBLK, 16), DBLK)


def block_lanes(index, width):
    return pl.ds(pl.multiple_of(index * width, 128), width)


def place_qkv_out(owner, start, piece, qkv_ref, out_ref):
    cut, stop = 3 * HALF_D, start + piece.shape[1]
    if start < cut:
        end = min(stop, cut)
        qkv_ref[block_rows(owner), start:end] = piece[:, : end - start]
    if stop > cut:
        begin = max(start, cut)
        lanes = pl.ds(pl.multiple_of(owner % 2 * HALF_D + (begin - cut), 128), stop - begin)
        out_ref[block_rows(owner // 2), lanes] = piece[:, begin - start :]


def place_gate_up(owner, start, piece, gate_ref, up_ref):
    stop = start + piece.shape[1]
    if start < HALF_FF:
        end = min(stop, HALF_FF)
        gate_ref[block_rows(owner), start:end] = piece[:, : end - start]
    if stop > HALF_FF:
        begin = max(start, HALF_FF)
        up_ref[block_rows(owner), begin - HALF_FF : stop - HALF_FF] = piece[:, begin - start :]


def place_down(owner, start, piece, out_ref):
    lanes = block_lanes(owner // 2, FBLK)
    for block in range(piece.shape[1] // FBLK):
        rows = block_rows(owner % 2 * HALF_GRID + start // FBLK + block)
        out_ref[rows, lanes] = piece[:, block * FBLK : (block + 1) * FBLK]


def assemble(me, high, sources, entries, place, shapes, name, begun=()):
    sources = list(sources)

    def kernel(me_ref, *refs):
        x, y, z = me_ref[0] % 2, me_ref[0] // 2 % 2, me_ref[0] // 4
        out_refs = refs[len(sources) + len(begun) :]
        for ref, out_ref in zip(refs[len(sources) :], out_refs if begun else ()):
            out_ref[...] = ref[...]
        for number, start, width, step, over_y, over_x, first in entries:
            slow = (z - step + high) % high
            from_y = 1 - y if over_y else y
            from_x = 1 - x if over_x else x
            piece = refs[number][:, start : start + width]
            place(slow * 4 + from_y * 2 + from_x, first, piece, *out_refs)

    return whole_call(
        kernel,
        [me] + sources + list(begun),
        [jax.ShapeDtypeStruct(shape, BF16) for shape in shapes],
        name,
        1,
    )


def pack_kernel(qkv_ref, out_ref, ffn_ref, down_ref, first_ref, second_ref, slab_ref, *scratch):
    held, sems = scratch[:-1], scratch[-1]
    copies = [
        pltpu.make_async_copy(ref, here, sems.at[number])
        for number, (ref, here) in enumerate(zip((qkv_ref, out_ref, ffn_ref, down_ref), held))
    ]
    for copy in copies:
        copy.start()

    def row(ref, matrix):
        return jnp.concatenate([ref[matrix, block].astype(BF16) for block in range(HALF_GRID)], 1)

    at = 0
    for copy, ref in zip(copies, held):
        copy.wait()
        for matrix in range(ref.shape[0]):
            part = row(ref, matrix)
            stop = at + part.shape[1]
            slab_ref[:, at:stop] = part
            if stop <= first_ref.shape[1]:
                first_ref[:, at:stop] = part
            elif stop <= first_ref.shape[1] + second_ref.shape[1]:
                second_ref[:, at - first_ref.shape[1] : stop - first_ref.shape[1]] = part
            at = stop


def pack(*masters):
    vmem = pl.BlockSpec(memory_space=pltpu.VMEM)
    return pl.pallas_call(
        pack_kernel,
        in_specs=[pl.BlockSpec(memory_space=pl.ANY)] * len(masters),
        out_specs=[vmem] * 3,
        out_shape=[
            jax.ShapeDtypeStruct((DBLK, width), BF16)
            for width in (4 * HALF_D, FF, 4 * HALF_D + 3 * HALF_FF)
        ],
        scratch_shapes=[pltpu.VMEM(master.shape, F32) for master in masters]
        + [pltpu.SemaphoreType.DMA((len(masters),))],
        compiler_params=kernel_params(PACK_MIB),
        cost_estimate=cost(),
        name="pack",
    )(*masters)


def tables_kernel(cos_ref, sin_ref, cosine_ref, sine_ref):
    cosine, sine = cos_ref[...], sin_ref[...]
    cosine_ref[...] = jnp.concatenate([cosine] * 4, 1)
    sine_ref[...] = jnp.concatenate([-sine, sine] * 2, 1)


def side_by_side(blocks):
    matrices, many, height, width = blocks.shape
    return blocks.transpose(2, 0, 1, 3).reshape(height, matrices * many * width)


def gather_by_name(qkv, out, ffn_part, down):
    qkv_all = lax.all_gather(qkv, "dp", axis=1, tiled=True)
    out_all = lax.all_gather(out[0], "dp", axis=0, tiled=True)
    ffn_all = lax.all_gather(ffn_part, "dp", axis=1, tiled=True)
    down_all = lax.all_gather(down, "dp", axis=0, tiled=True)
    w_qkv = qkv_all.reshape(3, GRID, HALF_GRID, DBLK, DBLK).transpose(1, 3, 0, 2, 4)
    w_out = out_all.reshape(HALF_GRID, GRID, DBLK, DBLK).transpose(0, 2, 1, 3)
    w_ffn = ffn_all.reshape(2, GRID, HALF_GRID, DBLK, FBLK).transpose(0, 1, 3, 2, 4)
    w_down = down_all.reshape(HALF_GRID, GRID, FBLK, DBLK).transpose(1, 3, 0, 2)
    w_ffn = w_ffn.reshape(2, D, HALF_FF)
    return (
        w_qkv.reshape(D, 3 * HALF_D),
        w_out.reshape(HALF_D, D),
        w_ffn[0],
        w_ffn[1],
        w_down.reshape(D, HALF_FF),
    )


def take_rows(owner, ref):
    return ref[block_rows(owner), :]


def take_out(owner, ref):
    return ref[block_rows(owner // 2), pl.ds(pl.multiple_of(owner % 2 * HALF_D, 128), HALF_D)]


def take_down(owner, ref):
    lanes = pl.ds(pl.multiple_of(owner // 2 * FBLK, 128), FBLK)
    return jnp.concatenate(
        [ref[block_rows(owner % 2 * HALF_GRID + block), lanes] for block in range(HALF_GRID)], 1
    )


def paired(values):
    high = values.astype(BF16)
    low = (values - high.astype(F32)).astype(BF16)
    rest = jnp.zeros((DBLK - 2 * values.shape[0], values.shape[1]), BF16)
    return jnp.concatenate([high, low, rest], 0)


def unpaired(pair):
    rows = STATE_ROWS
    return pair[:rows].astype(F32) + pair[rows : 2 * rows].astype(F32)


def reduction(takes, columns, count, me, grads):
    high = count // 4
    half = high // 2
    many = len(grads)

    def step(kernel, inputs, shapes, name):
        return whole_call(kernel, [me] + grads + inputs, shapes, name, 1)

    def find(refs, slow, y, x, part):
        owner = slow * 4 + y * 2 + x
        found = [take(owner, ref) for take, ref in zip(takes, refs)]
        found = found[0] if len(found) == 1 else jnp.concatenate(found, 1)
        return found[:, part[0] : part[1]].astype(F32)

    def place(me_ref):
        return me_ref[0] % 2, me_ref[0] // 2 % 2, me_ref[0] // 4

    def piece(index, width=columns, start=0, every=None):
        first = index * (every or width) + start
        return pl.ds(pl.multiple_of(first, 128), width)

    def diagonal_kernel(me_ref, *refs):
        x, y, _ = place(me_ref)
        *guest_refs, to_y_ref, to_x_ref = refs[many:]
        for guest_ref in guest_refs:
            wide = guest_ref.shape[1] // 4
            middle = 3 * wide + wide // 2
            to_y_ref[:, half * columns :] = guest_ref[:, 3 * wide : middle].astype(BF16)
            to_x_ref[:, half * columns :] = guest_ref[:, middle:].astype(BF16)

        @pl.loop(0, half)
        def _(step):
            whole = (0, columns)
            to_y_ref[:, piece(step)] = find(refs, step, 1 - y, 1 - x, whole).astype(BF16)
            to_x_ref[:, piece(step)] = find(refs, half + step, 1 - y, 1 - x, whole).astype(BF16)

    def side_kernel(part, me_ref, *refs):
        x, y, _ = place(me_ref)
        by_y_ref, by_x_ref, *state_refs, to_x_ref, to_y_ref = refs[many:]
        width = part[1] - part[0]
        if state_refs:
            guest_ref = state_refs[1]
            wide = guest_ref.shape[1] // 4
            cut, start = wide // 2, high * width + 128
            by_y = by_y_ref[:, half * columns :].astype(F32)
            by_x = by_x_ref[:, half * columns :].astype(F32)
            to_x_ref[:, start : start + cut] = (guest_ref[:, wide : wide + cut] + by_y).astype(BF16)
            to_x_ref[:, start + cut :] = guest_ref[:, wide + cut : 2 * wide].astype(BF16)
            start = high * width
            to_y_ref[:, start : start + cut] = guest_ref[:, 2 * wide : 2 * wide + cut].astype(BF16)
            to_y_ref[:, start + cut :] = (
                guest_ref[:, 2 * wide + cut : 3 * wide] + by_x
            ).astype(BF16)

        @pl.loop(0, half)
        def _(step):
            lanes = piece(step, width, part[0], columns)
            for slow, by_y, by_x in ((step, by_y_ref, None), (half + step, None, by_x_ref)):
                to_x = find(refs, slow, y, 1 - x, part)
                to_y = find(refs, slow, 1 - y, x, part)
                if by_y is not None:
                    to_x = to_x + by_y[:, lanes].astype(F32)
                else:
                    to_y = to_y + by_x[:, lanes].astype(F32)
                to_x_ref[:, piece(slow, width)] = to_x.astype(BF16)
                to_y_ref[:, piece(slow, width)] = to_y.astype(BF16)

        if state_refs:
            to_x_ref[:, high * width : high * width + 128] = paired(state_refs[0][...])

    def slow_kernel(part, me_ref, *refs):
        x, y, z = place(me_ref)
        from_x_ref, from_y_ref, *state_refs = refs[many : len(refs) - high]
        out_refs = refs[len(refs) - high :]
        width = part[1] - part[0]
        if state_refs:
            before_ref, after_ref = state_refs
            lanes = slice(high * width, high * width + 128)
            state = unpaired(paired(before_ref[...])) + unpaired(from_x_ref[:, lanes])
            after_ref[...] = state
        for shift in range(high):
            rows = pl.ds(0, DBLK)
            slow = (z + shift) % high
            lanes = pl.ds(pl.multiple_of(slow * width, 128), width)
            total = (
                find(refs, slow, y, x, part)
                + from_x_ref[rows, lanes].astype(F32)
                + from_y_ref[rows, lanes].astype(F32)
            )
            out_refs[shift][:, :width] = total.astype(out_refs[shift].dtype)
            if state_refs and shift:
                out_refs[shift][:, width:] = paired(state)

    def rows(width, kind=BF16):
        return jax.ShapeDtypeStruct((DBLK, width), kind)

    state_shape = jax.ShapeDtypeStruct((STATE_ROWS, 128), F32)

    def first(*guest):
        extra = sum(array.shape[1] // 8 for array in guest)
        shapes = [rows(half * columns + extra)] * 2
        return step(diagonal_kernel, list(guest), shapes, "send_diagonal")

    def second(by_y, by_x, *state, part=(0, columns)):
        wide = high * (part[1] - part[0])
        extra = state[1].shape[1] // 4 if state else 0
        shapes = [rows(wide + extra + (128 if state else 0)), rows(wide + extra)]
        kernel = functools.partial(side_kernel, part)
        return step(kernel, [by_y, by_x, *state], shapes, "send_sides")

    def third(from_x, from_y, *state, part=(0, columns)):
        width = part[1] - part[0]
        shapes = [state_shape] * len(state) + [rows(width, F32)]
        shapes += [rows(width + 128 * len(state))] * (high - 1)
        kernel = functools.partial(slow_kernel, part)
        return step(kernel, [from_x, from_y, *state], shapes, "send_slow")

    return first, second, third


def ring_blocks(grad, me, high):
    def kernel(me_ref, grad_ref, *out_refs):
        x, y, z = me_ref[0] % 2, me_ref[0] // 2 % 2, me_ref[0] // 4
        for hop, out_ref in enumerate(out_refs):
            slow = (z - 1 - hop + high) % high
            for part in range(4):
                from_x = 1 - x if part % 2 else x
                from_y = 1 - y if part // 2 else y
                block = take_down(slow * 4 + from_y * 2 + from_x, grad_ref)
                lanes = slice(part * HALF_FF, (part + 1) * HALF_FF)
                out_ref[:, lanes] = block.astype(out_ref.dtype)

    shapes = [
        jax.ShapeDtypeStruct((DBLK, 4 * HALF_FF), BF16 if hop < high - 1 else F32)
        for hop in range(high)
    ]
    return whole_call(kernel, [me, grad], shapes, "ring_blocks", 1)


def ring_add_kernel(far_ref, own_ref, out_ref):
    total = far_ref[...].astype(F32) + own_ref[...].astype(F32)
    out_ref[...] = total.astype(out_ref.dtype)


def ring_add(far, own):
    shape = jax.ShapeDtypeStruct(own.shape, own.dtype)
    return whole_call(ring_add_kernel, [far, own], [shape], "ring_add")[0]


def send_first(to_y, to_x, count):
    return along(to_y, 2, count), along(to_x, 1, count)


def send_second(to_x, to_y, count):
    return along(to_x, 1, count), along(to_y, 2, count)


def send_third(own, *others, count):
    return [own] + [shifted(block, step + 1, count) for step, block in enumerate(others)]


def scatter_all(qkv, out, ffn_grad, down, count):
    qkv = qkv.reshape(GRID, DBLK, 3, HALF_GRID, DBLK).transpose(2, 0, 3, 1, 4)
    out = out.reshape(HALF_GRID, DBLK, GRID, DBLK).transpose(0, 2, 1, 3)
    ffn_grad = ffn_grad.reshape(GRID, DBLK, 2, HALF_GRID, FBLK).transpose(2, 0, 3, 1, 4)
    down = down.reshape(GRID, DBLK, HALF_GRID, FBLK).transpose(2, 0, 3, 1)
    return (
        lax.psum_scatter(
            qkv.reshape(3, -1, DBLK, DBLK), "dp", scatter_dimension=1, tiled=True
        ),
        lax.psum_scatter(out.reshape(-1, DBLK, DBLK), "dp", scatter_dimension=0, tiled=True),
        lax.psum_scatter(
            ffn_grad.reshape(2, -1, DBLK, FBLK), "dp", scatter_dimension=1, tiled=True
        ),
        lax.psum_scatter(down.reshape(-1, FBLK, DBLK), "dp", scatter_dimension=0, tiled=True),
    )


def gain_rows_kernel(one_ref, two_ref, out_ref):
    def rows(values):
        return [values[:, at : at + 128] for at in range(0, D, 128)]

    parts = rows(one_ref[...]) + rows(0.5 * two_ref[...])
    parts.append(jnp.zeros((STATE_ROWS - len(parts), 128), F32))
    out_ref[...] = jnp.concatenate(parts, 0)


def gain_rows(gain_one, gain_two):
    shape = jax.ShapeDtypeStruct((STATE_ROWS, 128), F32)
    return whole_call(gain_rows_kernel, [gain_one, gain_two], [shape], "gain_rows")[0]


def add_kernel(left_ref, right_ref, out_ref):
    out_ref[...] = left_ref[...] + right_ref[...]


def added(left, right, name):
    return whole_call(add_kernel, [left, right], [jax.ShapeDtypeStruct(left.shape, F32)], name)[0]


def slow_state_kernel(own_ref, *refs):
    out_ref = refs[-1]
    columns = refs[0].shape[1] - 128
    values = [unpaired(paired(own_ref[...]))] + [unpaired(ref[:, columns:]) for ref in refs[:-1]]
    while len(values) > 1:
        half = len(values) // 2
        values = [values[index] + values[index + half] for index in range(half)]
    out_ref[...] = values[0]


def slow_state(own, blocks):
    shape = jax.ShapeDtypeStruct(own.shape, F32)
    return whole_call(slow_state_kernel, [own] + blocks, [shape], "slow_state")[0]


def gains_kernel(near_ref, far_ref, gain_ref, moment_ref, grad_ref, moment_new_ref, gain_new_ref):
    total = near_ref[...] + far_ref[...]
    count = D // 128
    grad = jnp.concatenate(
        [
            jnp.concatenate([total[at + row : at + row + 1] for row in range(count)], 1)
            for at in (0, count)
        ],
        0,
    )
    grad_ref[...] = grad
    moment = DECAY * moment_ref[...] + (1.0 - DECAY) * grad * grad
    moment_new_ref[...] = moment
    gain_new_ref[...] = gain_ref[...] - GAIN_RATE * grad / (jnp.sqrt(moment) + 1e-08)


def full_dot(left, right, left_dim, right_dim):
    return lax.dot_general(
        left,
        right,
        (((left_dim,), (right_dim,)), ((), ())),
        preferred_element_type=F32,
        precision=lax.Precision.DEFAULT,
    )


def precondition(
    parts,
    width,
    left,
    right,
    left_root,
    right_root,
    masters,
    turned=False,
    matrices=None,
    carry=(),
    starts=None,
):
    starts = [0] * len(parts) if starts is None else starts
    counts = [master.shape[0] for master in masters]
    spots = [(which, here) for which, many in enumerate(counts) for here in range(many)]
    matrices = range(len(spots)) if matrices is None else matrices
    many = len(parts)

    def kernel(*refs):
        part_refs, refs, total_ref = refs[:many], refs[many:-1], refs[-1]
        left_ref, right_ref, left_root_ref, right_root_ref = refs[:4]
        master_refs, refs = refs[4 : 4 + len(counts)], refs[4 + len(counts) :]
        carry_refs, refs = refs[: len(carry)], refs[len(carry) :]
        grad_ref, left_new_ref, right_new_ref = refs[:3]
        new_refs = refs[3:]
        for matrix, (which, here) in enumerate(spots):
            if carry and matrix not in matrices:
                for out_ref, carry_ref in zip(refs[:3], carry_refs[:3]):
                    out_ref[matrix] = carry_ref[matrix]
                new_refs[which][here] = carry_refs[3 + which][here]
        wide = len(matrices) * HALF_GRID * width
        total = jnp.zeros((part_refs[0].shape[0], wide), F32)
        for ref, start in zip(part_refs, starts):
            total = total + ref[:, start : start + wide].astype(F32)
        total_ref[...] = total

        def update(which, here, matrix, block, grad):
            grad_ref[matrix, block] = grad
            outer, inner = full_dot(grad, grad, 1, 1), full_dot(grad, grad, 0, 0)
            if turned:
                outer, inner = inner, outer
                step = full_dot(grad, left_root_ref[matrix, block], 1, 1)
                step = full_dot(right_root_ref[matrix, block], step, 0, 0)
            else:
                step = full_dot(left_root_ref[matrix, block], grad, 1, 0)
                step = full_dot(step, right_root_ref[matrix, block], 1, 0)
            left_new_ref[matrix, block] = DECAY * left_ref[matrix, block] + (1.0 - DECAY) * outer
            right_new_ref[matrix, block] = DECAY * right_ref[matrix, block] + (1.0 - DECAY) * inner
            new_refs[which][here, block] = master_refs[which][here, block] - STEP_RATE * step

        def update_matrix(which, here, matrix, number):
            start = number * HALF_GRID * width
            if width % 128:
                lanes = pl.ds(pl.multiple_of(start, 128), HALF_GRID * width)
                row = total_ref[:, lanes]
                for block in range(HALF_GRID):
                    at = block * width
                    update(which, here, matrix, block, row[:, at : at + width])
            else:

                @pl.loop(0, HALF_GRID // 4)
                def _(step):
                    for block in [4 * step + number for number in range(4)]:
                        lanes = pl.ds(pl.multiple_of(start + block * width, 128), width)
                        update(which, here, matrix, block, total_ref[:, lanes])

        if len({spots[matrix][0] for matrix in matrices}) == 1:

            @pl.loop(0, len(matrices))
            def _(number):
                matrix = number + matrices[0]
                update_matrix(spots[matrices[0]][0], number + spots[matrices[0]][1], matrix, number)
        else:
            for number, matrix in enumerate(matrices):
                update_matrix(*spots[matrix], matrix, number)

    grads = jax.ShapeDtypeStruct((sum(counts),) + masters[0].shape[1:], F32)
    like = [jax.ShapeDtypeStruct(array.shape, F32) for array in (left, right)]
    news = [jax.ShapeDtypeStruct(master.shape, F32) for master in masters]
    inputs = list(parts) + [left, right, left_root, right_root] + list(masters)
    total = pltpu.VMEM((parts[0].shape[0], len(matrices) * HALF_GRID * width), F32)
    return whole_call(
        kernel, inputs + list(carry), [grads] + like + news, "precondition", scratch=[total]
    )


def plain_precondition(block_grad, left_stat, right_stat, left_root, right_root, master):
    new_left = DECAY * left_stat + (1.0 - DECAY) * jnp.einsum(
        "...ij,...kj->...ik", block_grad, block_grad, precision=HIGHEST_PRECISION
    )
    new_right = DECAY * right_stat + (1.0 - DECAY) * jnp.einsum(
        "...ji,...jk->...ik", block_grad, block_grad, precision=HIGHEST_PRECISION
    )
    turned = jnp.einsum("...ij,...jk->...ik", left_root, block_grad, precision=HIGHEST_PRECISION)
    turned = jnp.einsum("...ij,...jk->...ik", turned, right_root, precision=HIGHEST_PRECISION)
    return (new_left, new_right, master - STEP_RATE * turned)


def in_order_kernel(core_ref, mine_ref, other_ref, out_ref):
    rows = mine_ref.shape[0]
    core = core_ref[0]
    out_ref[pl.ds(pl.multiple_of(core * rows, 16), rows), :] = mine_ref[...]
    out_ref[pl.ds(pl.multiple_of((1 - core) * rows, 16), rows), :] = other_ref[...]


def in_order(mine, core):
    shape = jax.ShapeDtypeStruct((2 * mine.shape[0], mine.shape[1]), mine.dtype)
    return whole_call(in_order_kernel, [core, mine, other_core(mine)], [shape], "in_order", 1)[0]


def own_and_all(core_ref, rows, step):
    own = pl.ds(pl.multiple_of(step * ROWS, ROWS), ROWS)
    return own, pl.ds(pl.multiple_of(core_ref[0] * rows + step * ROWS, ROWS), ROWS)


def layer_out_kernel(core_ref, x1_ref, near_ref, far_ref, out_ref):
    @pl.loop(0, out_ref.shape[0] // ROWS)
    def _(step):
        own, rows = own_and_all(core_ref, out_ref.shape[0], step)
        total = x1_ref[rows, :] + near_ref[rows, :].astype(F32) + far_ref[rows, :].astype(F32)
        out_ref[own, :] = total.astype(BF16)


def input_grad_kernel(core_ref, x_ref, dx1_ref, near_ref, far_ref, gain_ref, out_ref):
    @pl.loop(0, out_ref.shape[0] // ROWS)
    def _(step):
        own, rows = own_and_all(core_ref, out_ref.shape[0], step)
        x = x_ref[rows, :].astype(F32)
        scale = lax.rsqrt(jnp.mean(x * x, -1, keepdims=True) + EPSILON)
        grad = near_ref[rows, :].astype(F32) + far_ref[rows, :].astype(F32)
        weighted = grad * gain_ref[0:1, :]
        inner = jnp.mean(weighted * x, -1, keepdims=True)
        out_ref[own, :] = dx1_ref[rows, :] + scale * weighted - x * (scale * scale * scale * inner)


def rotary_tables(length):
    frequency = jnp.power(10000.0, -2.0 * jnp.arange(HEAD_DIM // 2, dtype=F32) / HEAD_DIM)
    angles = (jnp.arange(length) % LEN).astype(F32)[:, None] * frequency[None, :]
    shape = jax.ShapeDtypeStruct((length, PAIR), F32)
    return whole_call(tables_kernel, [jnp.cos(angles), jnp.sin(angles)], [shape] * 2, "tables")


def body(
    tokens,
    cotangent,
    gains,
    gain_moments,
    qkv_master,
    out_master,
    ffn_master,
    down_master,
    attn_left,
    attn_right,
    attn_left_root,
    attn_right_root,
    ffn_left,
    ffn_right,
    ffn_left_root,
    ffn_right_root,
    down_left,
    down_right,
    down_left_root,
    down_right_root,
):
    count = lax.axis_size("dp")
    me = lax.axis_index("dp").astype(jnp.int32)[None]
    core = lax.axis_index("narrow").astype(jnp.int32)[None]
    own_rows = tokens.shape[0]
    by_hand = count == GRID

    if by_hand:
        high = count // 4
        first, second, slab = pack(
            qkv_master[:, 0], out_master, ffn_master[:, 0], jnp.swapaxes(down_master, 2, 3)
        )
        one, two, last = 4 * HALF_D, FF, HALF_FF
        width, half, ring_start = one + two + last, (one + two + last) // 2, one + two
        many = high - 1
        far_one = all_shifted(first, count)
        slab_x, slab_y = along(slab, 1, count), along(slab, 2, count)

    x, cot = in_order(tokens, core), in_order(cotangent, core)
    cosine, sine_part = rotary_tables(x.shape[0])

    if by_hand:
        chunk = [(number, 0, one) for number in range(many)]
        near_x, near_y = copy_columns(
            [after(far_one[0], x, cot, cosine, sine_part)] + far_one[1:] + [slab_x, slab_y],
            [chunk + [(many + 1, half, width)], chunk + [(many, 0, half)]],
            "end_round_one",
        )
        one_x, one_y = along(near_x, 1, count), along(near_y, 2, count)
        far_two = all_shifted(after(second, *far_one), count)
        tail = many * one
        one_a, one_b, near_two, square = copy_columns(
            [one_x, one_y] + far_two + [slab, slab_x, slab_y],
            [
                [(0, number * one, number * one + one // 2) for number in range(many)],
                [(1, number * one + one // 2, (number + 1) * one) for number in range(many)],
                [(2 + number, 0, two) for number in range(many)],
                [(2 + many + part, ring_start, width) for part in range(3)]
                + [(0, tail + ring_start - half, tail + width - half)],
            ],
            "end_round_two",
        )
        one_a, one_b = along(one_a, 2, count), along(one_b, 1, count)
        squares = [square, shifted(square, 1, count)]
        entries = [(0, 0, one, 0, 0, 0, 0), (1, 0, one, 0, 0, 1, 0), (2, 0, one, 0, 1, 0, 0)]
        entries.append((5, tail, one, 0, 1, 1, 0))
        for number in range(many):
            step, at = number + 1, number * one
            entries += [(3, at, one, step, 0, 0, 0), (4, at, one, step, 0, 1, 0)]
            entries += [(5, at, one, step, 1, 0, 0)]
        shapes = [(D, 3 * HALF_D), (HALF_D, D)]
        early = [slab, slab_x, slab_y, near_x, one_x, one_y]
        early[0] = after(slab, near_two)
        w_early = assemble(me, high, early, entries, place_qkv_out, shapes, "place_qkv_out")
        entries = []
        for number in range(many):
            step, at = number + 1, number * (one // 2)
            entries += [(0, at, one // 2, step, 1, 1, 0), (1, at, one // 2, step, 1, 1, one // 2)]
        w_qkv, w_out = assemble(
            me, high, [one_a, one_b], entries, place_qkv_out, shapes, "place_rest", w_early
        )
        near_late = after(near_two, one_a, one_b, w_early[0], squares[1])
        two_x, two_y = along(near_late, 1, count), along(near_late, 2, count)
        squares.append(shifted(after(squares[1], one_a, one_b, w_early[0]), 1, count))
    else:
        qkv, ffn_part = qkv_master[:, 0].astype(BF16), ffn_master[:, 0].astype(BF16)
        w_qkv, w_out, w_gate, w_up, w_down = gather_by_name(
            qkv, out_master.astype(BF16), ffn_part, down_master[0].astype(BF16)
        )
    normed_one, q, k, v = project(x, gains, w_qkv, cosine, sine_part)
    attended, lse = attend(q, k, v)
    attended_late, w_out_late = attended, w_out
    if by_hand:
        two_a, two_b = copy_columns(
            [after(two_x, attended, *squares[1:]), two_y],
            [
                [(0, number * two, number * two + two // 2) for number in range(many)],
                [(1, number * two + two // 2, (number + 1) * two) for number in range(many)],
            ],
            "end_round_four",
        )
        early = [slab, slab_x, slab_y, one_x, one_y, near_two, two_x, two_y]
        early[0] = after(slab, two_a)
        attended_late, w_out_late = after(attended, two_a), after(w_out, two_a)
        two_a, two_b = along(two_a, 2, count), along(two_b, 1, count)
        cut = half - one
        entries = [(0, one, two, 0, 0, 0, 0), (1, one, two, 0, 0, 1, 0), (2, one, two, 0, 1, 0, 0)]
        entries += [(4, tail + one, cut, 0, 1, 1, 0), (3, tail, two - cut, 0, 1, 1, cut)]
        for number in range(many):
            step, at = number + 1, number * two
            entries += [(5, at, two, step, 0, 0, 0), (6, at, two, step, 0, 1, 0)]
            entries += [(7, at, two, step, 1, 0, 0)]
        shapes = [(D, HALF_FF)] * 2
        w_early = assemble(me, high, early, entries, place_gate_up, shapes, "place_gate_up")
        entries = []
        for number in range(many):
            step, at = number + 1, number * (two // 2)
            entries += [(0, at, two // 2, step, 1, 1, 0), (1, at, two // 2, step, 1, 1, two // 2)]
        w_gate, w_up = assemble(
            me,
            high,
            [two_a, two_b],
            entries,
            place_gate_up,
            shapes,
            "place_rest",
            w_early,
        )
        for _ in range(3, high):
            squares.append(shifted(after(squares[-1], w_gate), 1, count))
    attended_far, w_out_far = other_core(attended_late), other_core(w_out_late)
    middle, normed_two, gate, up, hidden = ffn(
        x, attended, attended_far, w_out, w_out_far, gains, w_gate, w_up
    )

    if by_hand:
        squares[0] = after(squares[0], hidden)
        (w_down,) = assemble(
            me,
            high,
            squares,
            [
                (step, part * last, last, step, part // 2, part % 2, 0)
                for step in range(high)
                for part in range(4)
            ],
            place_down,
            [(D, HALF_FF)],
            "place_down",
        )
    down_weight_grad = dot_tn(cot, hidden)
    cot_late = cot
    if by_hand:
        ring = ring_blocks(down_weight_grad, me, high)
        passed = shifted(ring[0], 1, count)
        cot_late = after(cot, ring[0])
    ffn_back_grad, normed_part = ffn_back(cot_late, gate, up, w_down, w_gate, w_up)
    if by_hand:
        sent = ring_add(after(passed, normed_part), ring[1])
        passed = shifted(sent, 1, count)
        ffn_back_grad = after(ffn_back_grad, sent)
        normed_part = after(normed_part, sent)
    normed_far = other_core(normed_part)
    ffn_weight_grad = dot_tn(normed_two, ffn_back_grad)
    if by_hand:
        ffn_sum = reduction([take_rows], FF, count, me, [ffn_weight_grad])
        sent = ffn_sum[0]()
        normed_far = after(normed_far, sent[0])
        ffn_far = send_first(*sent, count)
    middle_grad, branch, attended_grad, gain_two = middle_back(
        cot, middle, normed_part, normed_far, gains, w_out
    )
    out_weight_grad = dot_tn(attended, branch)
    out_part = ffn_out(after(hidden, branch), w_down)
    out_part_late = out_part
    if by_hand:
        late = [branch, out_part, out_weight_grad]
        for number in range(2, high - 1):
            sent = ring_add(after(passed, *late), ring[number])
            passed = shifted(sent, 1, count)
            late.append(sent)
        sent = ffn_sum[1](after(ffn_far[0], *late), ffn_far[1])
        ffn_far = send_second(*sent, count)
        attended_grad = after(attended_grad, sent[0])
        out_part_late = after(out_part, sent[0])
    out_far = other_core(out_part_late)
    qkv_back_grad = attend_back(q, k, v, attended_grad, attended, lse, cosine, sine_part)
    layer_out = whole_call(
        layer_out_kernel,
        [core, after(middle, qkv_back_grad), out_part, out_far],
        [jax.ShapeDtypeStruct((own_rows, D), BF16)],
        "layer_out",
        1,
    )[0]
    if by_hand:
        down_near = ring_add(after(passed, qkv_back_grad, layer_out), ring[-1])
        ffn_sent = ffn_sum[2](after(ffn_far[0], qkv_back_grad, layer_out), ffn_far[1])
        ffn_parts = [ffn_sent[0]] + [
            shifted(block, step + 1, count)
            for step, block in enumerate(ffn_sent[1:])
            if step + 1 != high // 2
        ]
        qkv_back_grad = after(qkv_back_grad, ffn_sent[0])
    qkv_weight_grad = dot_tn(normed_one, qkv_back_grad)
    if by_hand:
        late_sum = reduction(
            [take_rows, take_out], 4 * HALF_D, count, me, [qkv_weight_grad, out_weight_grad]
        )
        sent = late_sum[0](down_near)
        late_far = list(send_first(*sent, count))
        qkv_back_grad = after(qkv_back_grad, sent[0])
    input_part, gain_one = input_back(x, qkv_back_grad, w_qkv)
    input_part_late = input_part
    if by_hand:
        state = gain_rows(gain_one, gain_two)
        state = added(state, other_core(state), "add_gains")
        late_cut = 2 * HALF_D
        parts = [(0, late_cut), (late_cut, 2 * late_cut)]
        late_far[0] = after(late_far[0], *ffn_parts[1:])
        sent = late_sum[1](*late_far, state, down_near, part=parts[0])
        first_far = send_second(*sent, count)
        ffn_parts.append(shifted(after(ffn_sent[high // 2], sent[0]), high // 2, count))
        input_part_late = after(input_part, sent[0])
        second_sent = late_sum[1](after(late_far[0], sent[0]), late_far[1], part=parts[1])
    input_far = other_core(input_part_late)
    input_grad = whole_call(
        input_grad_kernel,
        [core, x, middle_grad, input_part, input_far, gains],
        [jax.ShapeDtypeStruct((own_rows, D), F32)],
        "input_grad",
        1,
    )[0]
    if by_hand:
        second_far = send_second(
            after(second_sent[0], input_grad, *first_far, *ffn_parts[1:]), second_sent[1], count
        )
        first_state, *sent = late_sum[2](
            *first_far,
            state,
            part=parts[0],
        )
        first_parts = send_third(*sent, count=count)
        ffn_parts[0] = after(ffn_parts[0], sent[0])
        ffn_grad, ffn_left_new, ffn_right_new, ffn_new = precondition(
            ffn_parts,
            FBLK,
            ffn_left[:, 0],
            ffn_right[:, 0],
            ffn_left_root[:, 0],
            ffn_right_root[:, 0],
            [ffn_master[:, 0]],
        )
        wide = high * late_cut
        down_grad, down_left_new, down_right_new, down_new = precondition(
            [after(down_near, ffn_left_new), *first_far],
            FBLK,
            down_left,
            down_right,
            down_left_root,
            down_right_root,
            [jnp.swapaxes(down_master, 2, 3)],
            turned=True,
            starts=[0, wide + 128, wide],
        )
        down_grad, down_new = jnp.swapaxes(down_grad, 2, 3), jnp.swapaxes(down_new, 2, 3)
        sent = late_sum[2](after(second_far[0], down_left_new), second_far[1], part=parts[1])
        second_parts = send_third(*sent, count=count)
        first_state = slow_state(after(first_state, sent[0]), first_parts[1:])
        first_parts[0] = after(first_parts[0], first_state)
        gain_grad, gain_moment_new, gain_new = whole_call(
            gains_kernel,
            [first_state, along(first_state, 2, count), gains, gain_moments],
            [jax.ShapeDtypeStruct(gains.shape, F32)] * 3,
            "gains",
        )
        attn_results = ()
        for matrices, some in ((range(2), first_parts), (range(2, 4), second_parts)):
            attn_results = precondition(
                some,
                DBLK,
                attn_left[:, 0],
                attn_right[:, 0],
                attn_left_root[:, 0],
                attn_right_root[:, 0],
                [qkv_master[:, 0], out_master],
                matrices=matrices,
                carry=attn_results,
            )
            second_parts[0] = after(second_parts[0], gain_grad, attn_results[0])
        *stacked, out_new = attn_results
        attn_grad, attn_left_new, attn_right_new, qkv_new = (array[:, None] for array in stacked)
        ffn_grad, ffn_left_new, ffn_right_new, ffn_new = (
            array[:, None] for array in (ffn_grad, ffn_left_new, ffn_right_new, ffn_new)
        )
    else:
        gain_terms = jnp.concatenate([gain_one, 0.5 * gain_two])
        gain_grad = lax.psum(gain_terms, ("dp", "narrow"))
        gain_moment_new = DECAY * gain_moments + (1.0 - DECAY) * gain_grad * gain_grad
        gain_new = gains - GAIN_RATE * gain_grad / (jnp.sqrt(gain_moment_new) + 1e-08)
        qkv_owned, out_owned, ffn_owned, down_owned = scatter_all(
            qkv_weight_grad, out_weight_grad, ffn_weight_grad, down_weight_grad, count
        )
        attn_grad = jnp.concatenate([qkv_owned, out_owned[None]], 0)[:, None]
        ffn_grad = ffn_owned[:, None]
        down_grad = down_owned[None]
        attn_left_new, attn_right_new, attn_new = plain_precondition(
            attn_grad,
            attn_left,
            attn_right,
            attn_left_root,
            attn_right_root,
            jnp.concatenate([qkv_master, out_master[None]], 0),
        )
        qkv_new, out_new = attn_new[:3], attn_new[3]
        ffn_left_new, ffn_right_new, ffn_new = plain_precondition(
            ffn_grad, ffn_left, ffn_right, ffn_left_root, ffn_right_root, ffn_master
        )
        down_left_new, down_right_new, down_new = plain_precondition(
            down_grad, down_left, down_right, down_left_root, down_right_root, down_master
        )
    return (
        layer_out,
        input_grad,
        gain_grad,
        gain_moment_new,
        gain_new,
        attn_grad,
        attn_left_new,
        attn_right_new,
        qkv_new,
        out_new,
        ffn_grad,
        ffn_left_new,
        ffn_right_new,
        ffn_new,
        down_grad,
        down_left_new,
        down_right_new,
        down_new,
    )


def solution(mesh):
    tokens = P(("dp", "narrow"), None)
    stacked = P(None, "narrow", "dp", None, None)
    single = P("narrow", "dp", None, None)
    return jax.shard_map(
        body,
        mesh=mesh,
        in_specs=(tokens, tokens, P(), P(), stacked, single, stacked, single)
        + (stacked,) * 8
        + (single,) * 4,
        out_specs=(tokens, tokens, P(), P(), P())
        + (stacked,) * 4
        + (single,)
        + (stacked,) * 4
        + (single,) * 4,
        check_vma=False,
    )
```

profile of v0, /device:TPU:0, one launch (start us, length us, event | category | flops | bytes accessed | tf_op | source)
XLA Modules:
  0.0 202.1 jit_solution(13594446178878486690)
XLA Ops:
  1.3 2.3 %pack.1 = (bf16[48,1536]{1,0:T(8,128)(2,1)}, bf16[48,2048]{1,0:T(8,128)(2,1)}, bf16[48,4608]{1,0:T(8,128)(2,1)}) custom-call(f32[3,8,48,48]{3,2,1,0:T(8,128)} %bitcast.47, f32[1,8,48,48]{3,2,1,0:T(8,128)} %refs_9_.3, f32[2,8,48,128]{3,2,1,0:T(8,128)} %bitcast.58, f32[1,8,48,128]{3,2,1,0:T(8,128)} %bitcast.62), custom_call_target="tpu_custom_call" | custom-call | tf_op jit(solution)/shard_map/pack/pallas_call | solution.py:532
  3.6 3.0 %collective-permute-start.6 = (bf16[48,4608]{1,0:T(8,128)(2,1)}, bf16[48,4608]{1,0:T(8,128)(2,1)}, u32[]{:S(2)}, u32[]{:S(2)}) collective-permute-start(bf16[48,4608]{1,0:T(8,128)(2,1)} %get-tuple-element.172.refs_5_.refs_0_), channel_id=1, source_target_pairs={{0,4},{2,6},{4,0},{6,2},{8,12},{10,14},{12,8},{14,10},{16,20},{18,... | collective-permute-start | bytes 1327112 | tf_op jit(solution)/shard_map/ppermute | solution.py:412
  8.1 3.6 %collective-permute-start.4 = (bf16[48,1536]{1,0:T(8,128)(2,1)}, bf16[48,1536]{1,0:T(8,128)(2,1)S(1)}, u32[]{:S(2)}, u32[]{:S(2)}) collective-permute-start(bf16[48,1536]{1,0:T(8,128)(2,1)} %get-tuple-element.143), channel_id=1, source_target_pairs={{0,24},{2,26},{4,28},{6,30},{8,0},{10,2},{12,4},{14,6},{16,8},{18,... | collective-permute-start | bytes 442376 | tf_op jit(solution)/shard_map/ppermute | solution.py:416
  18.7 3.3 %collective-permute-done.1.refs_0_ = bf16[48,1536]{1,0:T(8,128)(2,1)S(1)} collective-permute-done((bf16[48,1536]{1,0:T(8,128)(2,1)}, bf16[48,1536]{1,0:T(8,128)(2,1)S(1)}, u32[]{:S(2)}, u32[]{:S(2)}) %collective-permute-start.1) | collective-permute-done | bytes 147488 | tf_op jit(solution)/shard_map/ppermute | solution.py:416
  33.1 12.6 %collective-permute-done.10.refs_3_ = bf16[48,2048]{1,0:T(8,128)(2,1)S(1)} collective-permute-done((bf16[48,2048]{1,0:T(8,128)(2,1)S(1)}, bf16[48,2048]{1,0:T(8,128)(2,1)S(1)}, u32[]{:S(2)}, u32[]{:S(2)}) %collective-permute-start.10) | collective-permute-done | bytes 196640 | tf_op jit(solution)/shard_map/ppermute | solution.py:416
  45.8 2.4 %end_round_two.1 = (bf16[48,2304]{1,0:T(8,128)(2,1)}, bf16[48,2304]{1,0:T(8,128)(2,1)}, bf16[48,6144]{1,0:T(8,128)(2,1)S(1)}, bf16[48,4096]{1,0:T(8,128)(2,1)S(1)}) custom-call(bf16[48,6912]{1,0:T(8,128)(2,1)S(1)} %collective-permute-done.7.refs_0_.refs_4_.refs_3_, bf16[48,6912]{1,0:T(8,128)(2,1)S(1)} %collective-permute-done.8.refs_1_.refs_5_.refs_4_, ...), custom_call_target="tpu_custom_call" | custom-call | tf_op jit(solution)/shard_map/end_round_two/pallas_call | solution.py:64
  64.4 2.9 %project.1 = (bf16[1024,768]{1,0:T(8,128)(2,1)S(1)}, bf16[1024,384]{1,0:T(8,128)(2,1)S(1)}, bf16[1024,384]{1,0:T(8,128)(2,1)S(1)}, bf16[1024,384]{1,0:T(8,128)(2,1)S(1)}) custom-call(bf16[1024,768]{1,0:T(8,128)(2,1)S(1)} %in_order.2.x_ref, f32[2,768]{1,0:T(2,128)S(1)} %copy-done.47, bf16[768,1152]{1,0:T(8,128)(2,1)S(1)} %get-tuple-element.158.w_ref, ...), custom_call_target="tpu_custom_call" | custom-call | tf_op jit(solution)/shard_map/project/pallas_call | solution.py:64
  67.3 7.8 %attend.1 = (bf16[1024,384]{1,0:T(8,128)(2,1)S(1)}, f32[24,1024]{1,0:T(8,128)S(1)}) custom-call(bf16[1024,384]{1,0:T(8,128)(2,1)S(1)} %get-tuple-element.159.q_ref, bf16[1024,384]{1,0:T(8,128)(2,1)S(1)} %get-tuple-element.160.k_ref, bf16[1024,384]{1,0:T(8,128)(2,1)S(1)} %get-tuple-element.161.v_ref), custom_call_target="tpu_custom_call" | custom-call | tf_op jit(solution)/shard_map/attend/pallas_call | solution.py:64
  78.2 6.6 %collective-permute-done.21.refs_1_ = bf16[48,3072]{1,0:T(8,128)(2,1)S(1)} collective-permute-done((bf16[48,3072]{1,0:T(8,128)(2,1)S(1)}, bf16[48,3072]{1,0:T(8,128)(2,1)S(1)}, u32[]{:S(2)}, u32[]{:S(2)}) %collective-permute-start.21) | collective-permute-done | bytes 294944 | tf_op jit(solution)/shard_map/ppermute | solution.py:412
  86.7 7.1 %ffn.1 = (f32[1024,768]{1,0:T(8,128)S(1)}, bf16[1024,768]{1,0:T(8,128)(2,1)S(1)}, f32[1024,1024]{1,0:T(8,128)S(1)}, f32[1024,1024]{1,0:T(8,128)S(1)}, bf16[1024,1024]{1,0:T(8,128)(2,1)S(1)}) custom-call(bf16[1024,768]{1,0:T(8,128)(2,1)S(1)} %in_order.2.x_ref, bf16[1024,384]{1,0:T(8,128)(2,1)S(1)} %get-tuple-element.168.o_ref, ...), custom_call_target="tpu_custom_call" | custom-call | tf_op jit(solution)/shard_map/ffn/pallas_call | solution.py:64
  99.1 8.1 %ffn_back.1 = (bf16[1024,2048]{1,0:T(8,128)(2,1)S(1)}, bf16[1024,768]{1,0:T(8,128)(2,1)S(1)}) custom-call(bf16[1024,768]{1,0:T(8,128)(2,1)S(1)} %in_order.3.cot_ref, f32[1024,1024]{1,0:T(8,128)S(1)} %get-tuple-element.181.gate_ref, f32[1024,1024]{1,0:T(8,128)S(1)} %get-tuple-element.182.up_ref, bf16[768,1024]{1,0:T(8,128)(2,1)S(1)} %place_down.1.wdt_ref, ...), custom_call_target="tpu_custom_call" | custom-call | tf_op jit(solution)/shard_map/ffn_back/pallas_call | solution.py:64
  109.9 3.6 %fusion.5.refs_0_ = f32[768,2048]{1,0:T(8,128)S(1)} fusion(bf16[1024,768]{1,0:T(8,128)(2,1)S(1)} %get-tuple-element.189, bf16[1024,2048]{1,0:T(8,128)(2,1)S(1)} %get-tuple-element.191), kind=kOutput, calls=%fused_computation.10 | convolution fusion | flops 3221225472 | bytes 12058624 | tf_op jit(solution)/shard_map/dot_general | solution.py:50
  115.6 2.5 %middle_back.1 = (f32[1024,768]{1,0:T(8,128)S(1)}, bf16[1024,768]{1,0:T(8,128)(2,1)S(1)}, bf16[1024,384]{1,0:T(8,128)(2,1)S(1)}, f32[1,768]{1,0:T(1,128)S(1)}) custom-call(bf16[1024,768]{1,0:T(8,128)(2,1)S(1)} %in_order.3.cot_ref, f32[1024,768]{1,0:T(8,128)S(1)} %get-tuple-element.204.x1_ref, bf16[1024,768]{1,0:T(8,128)(2,1)S(1)} %get-tuple-element.188.near_ref, ...), custom_call_target="tpu_custom_call" | custom-call | tf_op jit(solution)/shard_map/middle_back/pallas_call | solution.py:64
  121.4 3.4 %collective-permute-done.25.refs_1_ = bf16[48,4096]{1,0:T(8,128)(2,1)S(1)} collective-permute-done((bf16[48,4096]{1,0:T(8,128)(2,1)S(1)}, bf16[48,4096]{1,0:T(8,128)(2,1)S(1)}, u32[]{:S(2)}, u32[]{:S(2)}) %collective-permute-start.25) | collective-permute-done | bytes 393248 | tf_op jit(solution)/shard_map/ppermute | solution.py:412
  128.9 14.0 %attend_back.1.dqkv_ref = bf16[1024,1152]{1,0:T(8,128)(2,1)S(1)} custom-call(bf16[1024,384]{1,0:T(8,128)(2,1)S(1)} %get-tuple-element.159.q_ref, bf16[1024,384]{1,0:T(8,128)(2,1)S(1)} %get-tuple-element.160.k_ref, bf16[1024,384]{1,0:T(8,128)(2,1)S(1)} %copy-done.11, bf16[1024,384]{1,0:T(8,128)(2,1)S(1)} %get-tuple-element.202.do_ref, ...), custom_call_target="tpu_custom_call" | custom-call | tf_op jit(solution)/shard_map/attend_back/pallas_call | solution.py:64
  153.2 3.4 %collective-permute-start.34 = (bf16[48,2048]{1,0:T(8,128)(2,1)S(1)}, bf16[48,2048]{1,0:T(8,128)(2,1)S(1)}, u32[]{:S(2)}, u32[]{:S(2)}) collective-permute-start(bf16[48,2048]{1,0:T(8,128)(2,1)S(1)} %get-tuple-element.218), channel_id=1, source_target_pairs={{0,24},{2,26},{4,28},{6,30},{8,0},{10,2},{12,4},{14,6},{16,8},{18,... | collective-permute-start | bytes 589832 | tf_op jit(solution)/shard_map/ppermute | solution.py:416
  156.6 2.5 %input_back.1 = (bf16[1024,768]{1,0:T(8,128)(2,1)S(1)}, f32[1,768]{1,0:T(1,128)S(1)}) custom-call(bf16[1024,768]{1,0:T(8,128)(2,1)S(1)} %in_order.2.x_ref, bf16[1024,1152]{1,0:T(8,128)(2,1)S(1)} %attend_back.1.dqkv_ref, bf16[768,1152]{1,0:T(8,128)(2,1)S(1)} %get-tuple-element.158.w_ref), custom_call_target="tpu_custom_call" | custom-call | tf_op jit(solution)/shard_map/input_back/pallas_call | solution.py:64
  169.3 7.4 %collective-permute-done.40.refs_3_ = bf16[48,2048]{1,0:T(8,128)(2,1)S(1)} collective-permute-done((bf16[48,2048]{1,0:T(8,128)(2,1)S(1)}, bf16[48,2048]{1,0:T(8,128)(2,1)S(1)}, u32[]{:S(2)}, u32[]{:S(2)}) %collective-permute-start.40) | collective-permute-done | bytes 196640 | tf_op jit(solution)/shard_map/ppermute | solution.py:416
  179.2 2.7 %collective-permute-start.44 = (bf16[48,896]{1,0:T(8,128)(2,1)S(1)}, bf16[48,896]{1,0:T(8,128)(2,1)S(1)}, u32[]{:S(2)}, u32[]{:S(2)}) collective-permute-start(bf16[48,896]{1,0:T(8,128)(2,1)S(1)} %get-tuple-element.242), channel_id=1, source_target_pairs={{0,16},{2,18},{4,20},{6,22},{8,24},{10,26},{12,28},{14,30},{16,0},... | collective-permute-start | bytes 258056 | tf_op jit(solution)/shard_map/ppermute | solution.py:416
  183.1 3.1 %precondition.4 = (f32[2,8,48,128]{3,2,1,0:T(8,128)}, f32[2,8,48,48]{3,2,1,0:T(8,128)}, f32[2,8,128,128]{3,2,1,0:T(8,128)}, f32[2,8,48,128]{3,2,1,0:T(8,128)}) custom-call(f32[48,2048]{1,0:T(8,128)S(1)} %get-tuple-element.233.refs_0_, bf16[48,2048]{1,0:T(8,128)(2,1)S(1)} %collective-permute-done.33.refs_1_, ...), custom_call_target="tpu_custom_call" | custom-call | tf_op jit(solution)/shard_map/precondition/pallas_call | solution.py:64
  186.2 2.6 %precondition.5 = (f32[1,8,48,128]{3,2,1,0:T(8,128)}, f32[1,8,128,128]{3,2,1,0:T(8,128)}, f32[1,8,48,48]{3,2,1,0:T(8,128)}, f32[1,8,48,128]{3,2,1,0:T(8,128)}) custom-call(f32[48,4096]{1,0:T(8,128)S(1)} %ring_add.5.refs_2_.refs_5_.refs_0_, bf16[48,4224]{1,0:T(8,128)(2,1)S(1)} %collective-permute-done.38.refs_2_.refs_1_, ...), custom_call_target="tpu_custom_call" | custom-call | tf_op jit(solution)/shard_map/precondition/pallas_call | solution.py:64
  191.2 2.8 %collective-permute-start.49 = (bf16[48,768]{1,0:T(8,128)(2,1)S(1)}, bf16[48,768]{1,0:T(8,128)(2,1)S(1)}, u32[]{:S(2)}, u32[]{:S(2)}) collective-permute-start(bf16[48,768]{1,0:T(8,128)(2,1)S(1)} %get-tuple-element.252), channel_id=1, source_target_pairs={{0,24},{2,26},{4,28},{6,30},{8,0},{10,2},{12,4},{14,6},{16,8},{18,... | collective-permute-start | bytes 221192 | tf_op jit(solution)/shard_map/ppermute | solution.py:416
  194.7 2.4 %precondition.6 = (f32[4,8,48,48]{3,2,1,0:T(8,128)S(1)}, f32[4,8,48,48]{3,2,1,0:T(8,128)S(1)}, f32[4,8,48,48]{3,2,1,0:T(8,128)S(1)}, f32[3,8,48,48]{3,2,1,0:T(8,128)S(1)}, f32[1,8,48,48]{3,2,1,0:T(8,128)S(1)}) custom-call(f32[48,768]{1,0:T(8,128)S(1)} %get-tuple-element.247.refs_0_, bf16[48,896]{1,0:T(8,128)(2,1)S(1)} %collective-permute-done.43.refs_0_.refs_1_, ...), custom_call_target="tpu_custom_call" | custom-call | tf_op jit(solution)/shard_map/precondition/pallas_call | solution.py:64
  198.4 3.8 %precondition.7 = (f32[4,8,48,48]{3,2,1,0:T(8,128)}, f32[4,8,48,48]{3,2,1,0:T(8,128)}, f32[4,8,48,48]{3,2,1,0:T(8,128)}, f32[3,8,48,48]{3,2,1,0:T(8,128)}, f32[1,8,48,48]{3,2,1,0:T(8,128)}) custom-call(f32[48,768]{1,0:T(8,128)S(1)} %get-tuple-element.249.refs_0_, bf16[48,768]{1,0:T(8,128)(2,1)S(1)} %collective-permute-done.47.refs_1_, ...), custom_call_target="tpu_custom_call" | custom-call | tf_op jit(solution)/shard_map/precondition/pallas_call | solution.py:64
  (225 shorter events, 86.7 us)
Async XLA Ops:
  3.6 20.5 %collective-permute-start.6 = (bf16[48,4608]{1,0:T(8,128)(2,1)}, bf16[48,4608]{1,0:T(8,128)(2,1)}, u32[]{:S(2)}, u32[]{:S(2)}) collective-permute-start(bf16[48,4608]{1,0:T(8,128)(2,1)} %get-tuple-element.172.refs_5_.refs_0_), channel_id=1, source_target_pairs={{0,4},{2,6},{4,0},{6,2},{8,12},{10,14},{12,8},{14,10},{16,20},{18,... | collective-permute-start | bytes 1327112 | tf_op jit(solution)/shard_map/ppermute | solution.py:412
  6.6 17.5 %collective-permute-start.5 = (bf16[48,4608]{1,0:T(8,128)(2,1)}, bf16[48,4608]{1,0:T(8,128)(2,1)}, u32[]{:S(2)}, u32[]{:S(2)}) collective-permute-start(bf16[48,4608]{1,0:T(8,128)(2,1)} %get-tuple-element.172.refs_5_.refs_0_), channel_id=1, source_target_pairs={{0,2},{2,0},{4,6},{6,4},{8,10},{10,8},{12,14},{14,12},{16,18},{18,... | collective-permute-start | bytes 1327112 | tf_op jit(solution)/shard_map/ppermute | solution.py:412
  8.1 13.9 %collective-permute-start.4 = (bf16[48,1536]{1,0:T(8,128)(2,1)}, bf16[48,1536]{1,0:T(8,128)(2,1)S(1)}, u32[]{:S(2)}, u32[]{:S(2)}) collective-permute-start(bf16[48,1536]{1,0:T(8,128)(2,1)} %get-tuple-element.143), channel_id=1, source_target_pairs={{0,24},{2,26},{4,28},{6,30},{8,0},{10,2},{12,4},{14,6},{16,8},{18,... | collective-permute-start | bytes 442376 | tf_op jit(solution)/shard_map/ppermute | solution.py:416
  11.7 12.3 %collective-permute-start.3 = (bf16[48,1536]{1,0:T(8,128)(2,1)}, bf16[48,1536]{1,0:T(8,128)(2,1)S(1)}, u32[]{:S(2)}, u32[]{:S(2)}) collective-permute-start(bf16[48,1536]{1,0:T(8,128)(2,1)} %get-tuple-element.143), channel_id=1, source_target_pairs={{0,16},{2,18},{4,20},{6,22},{8,24},{10,26},{12,28},{14,30},{16,0},... | collective-permute-start | bytes 442376 | tf_op jit(solution)/shard_map/ppermute | solution.py:416
  25.3 20.4 %collective-permute-start.8 = (bf16[48,6912]{1,0:T(8,128)(2,1)S(1)}, bf16[48,6912]{1,0:T(8,128)(2,1)S(1)}, u32[]{:S(2)}, u32[]{:S(2)}) collective-permute-start(bf16[48,6912]{1,0:T(8,128)(2,1)S(1)} %get-tuple-element.149), channel_id=1, source_target_pairs={{0,4},{2,6},{4,0},{6,2},{8,12},{10,14},{12,8},{14,10},{16,20},{18,... | collective-permute-start | bytes 1990664 | tf_op jit(solution)/shard_map/ppermute | solution.py:412
  25.9 19.9 %collective-permute-start.7 = (bf16[48,6912]{1,0:T(8,128)(2,1)S(1)}, bf16[48,6912]{1,0:T(8,128)(2,1)S(1)}, u32[]{:S(2)}, u32[]{:S(2)}) collective-permute-start(bf16[48,6912]{1,0:T(8,128)(2,1)S(1)} %get-tuple-element.148.refs_3_), channel_id=1, source_target_pairs={{0,2},{2,0},{4,6},{6,4},{8,10},{10,8},{12,14},{14,12},{16,18},{18,... | collective-permute-start | bytes 1990664 | tf_op jit(solution)/shard_map/ppermute | solution.py:412
  27.8 17.9 %collective-permute-start.10 = (bf16[48,2048]{1,0:T(8,128)(2,1)S(1)}, bf16[48,2048]{1,0:T(8,128)(2,1)S(1)}, u32[]{:S(2)}, u32[]{:S(2)}) collective-permute-start(bf16[48,2048]{1,0:T(8,128)(2,1)S(1)} %copy-done.49), channel_id=1, source_target_pairs={{0,16},{2,18},{4,20},{6,22},{8,24},{10,26},{12,28},{14,30},{16,0},... | collective-permute-start | bytes 589832 | tf_op jit(solution)/shard_map/ppermute | solution.py:416
  29.3 16.5 %collective-permute-start.9 = (bf16[48,2048]{1,0:T(8,128)(2,1)S(1)}, bf16[48,2048]{1,0:T(8,128)(2,1)S(1)}, u32[]{:S(2)}, u32[]{:S(2)}) collective-permute-start(bf16[48,2048]{1,0:T(8,128)(2,1)S(1)} %copy-done.49), channel_id=1, source_target_pairs={{0,8},{2,10},{4,12},{6,14},{8,16},{10,18},{12,20},{14,22},{16,24},... | collective-permute-start | bytes 589832 | tf_op jit(solution)/shard_map/ppermute | solution.py:416
  60.1 15.1 %collective-permute-start.15 = (bf16[48,6144]{1,0:T(8,128)(2,1)S(1)}, bf16[48,6144]{1,0:T(8,128)(2,1)S(1)}, u32[]{:S(2)}, u32[]{:S(2)}) collective-permute-start(bf16[48,6144]{1,0:T(8,128)(2,1)S(1)} %copy-done.38), channel_id=1, source_target_pairs={{0,2},{2,0},{4,6},{6,4},{8,10},{10,8},{12,14},{14,12},{16,18},{18,... | collective-permute-start | bytes 1769480 | tf_op jit(solution)/shard_map/ppermute | solution.py:412
  61.6 13.6 %collective-permute-start.17 = (bf16[48,6144]{1,0:T(8,128)(2,1)S(1)}, bf16[48,6144]{1,0:T(8,128)(2,1)S(1)}, u32[]{:S(2)}, u32[]{:S(2)}) collective-permute-start(bf16[48,6144]{1,0:T(8,128)(2,1)S(1)} %copy-done.38), channel_id=1, source_target_pairs={{0,4},{2,6},{4,0},{6,2},{8,12},{10,14},{12,8},{14,10},{16,20},{18,... | collective-permute-start | bytes 1769480 | tf_op jit(solution)/shard_map/ppermute | solution.py:412
  63.1 12.1 %collective-permute-start.16 = (bf16[48,4096]{1,0:T(8,128)(2,1)}, bf16[48,4096]{1,0:T(8,128)(2,1)S(1)}, u32[]{:S(2)}, u32[]{:S(2)}) collective-permute-start(bf16[48,4096]{1,0:T(8,128)(2,1)} %collective-permute-done.14.refs_1_), channel_id=1, source_target_pairs={{0,8},{2,10},{4,12},{6,14},{8,16},{10,18},{12,20},{14,22},{16,24},... | collective-permute-start | bytes 1179656 | tf_op jit(solution)/shard_map/ppermute | solution.py:416
  85.3 12.3 %collective-permute-start.22 = (bf16[48,4096]{1,0:T(8,128)(2,1)S(1)}, bf16[48,4096]{1,0:T(8,128)(2,1)S(1)}, u32[]{:S(2)}, u32[]{:S(2)}) collective-permute-start(bf16[48,4096]{1,0:T(8,128)(2,1)S(1)} %collective-permute-done.16.refs_2_), channel_id=1, source_target_pairs={{0,8},{2,10},{4,12},{6,14},{8,16},{10,18},{12,20},{14,22},{16,24},... | collective-permute-start | bytes 1179656 | tf_op jit(solution)/shard_map/ppermute | solution.py:416
  108.0 13.3 %collective-permute-start.26 = (bf16[48,4096]{1,0:T(8,128)(2,1)S(1)}, bf16[48,4096]{1,0:T(8,128)(2,1)S(1)}, u32[]{:S(2)}, u32[]{:S(2)}) collective-permute-start(bf16[48,4096]{1,0:T(8,128)(2,1)S(1)} %ring_add.3), channel_id=1, source_target_pairs={{0,8},{2,10},{4,12},{6,14},{8,16},{10,18},{12,20},{14,22},{16,24},... | collective-permute-start | bytes 1179656 | tf_op jit(solution)/shard_map/ppermute | solution.py:416
  125.3 17.6 %collective-permute-start.28 = (bf16[1024,768]{1,0:T(8,128)(2,1)S(1)}, bf16[1024,768]{1,0:T(8,128)(2,1)S(1)}, u32[]{:S(2)}, u32[]{:S(2)}) collective-permute-start(bf16[1024,768]{1,0:T(8,128)(2,1)S(1)} %ffn_out.1.near_ref), channel_id=1, source_target_pairs={{0,1},{1,0},{2,3},{3,2},{4,5},{5,4},{6,7},{7,6},{8,9},{9,8},{10,11... | collective-permute-start | bytes 4718600 | tf_op jit(solution)/shard_map/ppermute | solution.py:420
  125.4 20.0 %collective-permute-start.29 = (bf16[48,8192]{1,0:T(8,128)(2,1)S(1)}, bf16[48,8192]{1,0:T(8,128)(2,1)S(1)}, u32[]{:S(2)}, u32[]{:S(2)}) collective-permute-start(bf16[48,8192]{1,0:T(8,128)(2,1)S(1)} %get-tuple-element.201), channel_id=1, source_target_pairs={{0,2},{2,0},{4,6},{6,4},{8,10},{10,8},{12,14},{14,12},{16,18},{18,... | collective-permute-start | bytes 2359304 | tf_op jit(solution)/shard_map/ppermute | solution.py:412
  126.9 19.6 %collective-permute-start.30 = (bf16[48,8192]{1,0:T(8,128)(2,1)S(1)}, bf16[48,8192]{1,0:T(8,128)(2,1)S(1)}, u32[]{:S(2)}, u32[]{:S(2)}) collective-permute-start(bf16[48,8192]{1,0:T(8,128)(2,1)S(1)} %get-tuple-element.208), channel_id=1, source_target_pairs={{0,4},{2,6},{4,0},{6,2},{8,12},{10,14},{12,8},{14,10},{16,20},{18,... | collective-permute-start | bytes 2359304 | tf_op jit(solution)/shard_map/ppermute | solution.py:412
  128.4 15.6 %collective-permute-start.31 = (bf16[48,4096]{1,0:T(8,128)(2,1)S(1)}, bf16[48,4096]{1,0:T(8,128)(2,1)S(1)}, u32[]{:S(2)}, u32[]{:S(2)}) collective-permute-start(bf16[48,4096]{1,0:T(8,128)(2,1)S(1)} %ring_add.4), channel_id=1, source_target_pairs={{0,8},{2,10},{4,12},{6,14},{8,16},{10,18},{12,20},{14,22},{16,24},... | collective-permute-start | bytes 1179656 | tf_op jit(solution)/shard_map/ppermute | solution.py:416
  150.6 12.1 %collective-permute-start.32 = (bf16[48,3584]{1,0:T(8,128)(2,1)S(1)}, bf16[48,3584]{1,0:T(8,128)(2,1)S(1)}, u32[]{:S(2)}, u32[]{:S(2)}) collective-permute-start(bf16[48,3584]{1,0:T(8,128)(2,1)S(1)} %get-tuple-element.214), channel_id=1, source_target_pairs={{0,4},{2,6},{4,0},{6,2},{8,12},{10,14},{12,8},{14,10},{16,20},{18,... | collective-permute-start | bytes 1032200 | tf_op jit(solution)/shard_map/ppermute | solution.py:412
  163.0 13.8 %collective-permute-start.38 = (bf16[48,4224]{1,0:T(8,128)(2,1)S(1)}, bf16[48,4224]{1,0:T(8,128)(2,1)S(1)}, u32[]{:S(2)}, u32[]{:S(2)}) collective-permute-start(bf16[48,4224]{1,0:T(8,128)(2,1)S(1)} %get-tuple-element.223), channel_id=1, source_target_pairs={{0,2},{2,0},{4,6},{6,4},{8,10},{10,8},{12,14},{14,12},{16,18},{18,... | collective-permute-start | bytes 1216520 | tf_op jit(solution)/shard_map/ppermute | solution.py:412
  164.4 12.3 %collective-permute-start.39 = (bf16[48,4096]{1,0:T(8,128)(2,1)S(1)}, bf16[48,4096]{1,0:T(8,128)(2,1)S(1)}, u32[]{:S(2)}, u32[]{:S(2)}) collective-permute-start(bf16[48,4096]{1,0:T(8,128)(2,1)S(1)} %get-tuple-element.225), channel_id=1, source_target_pairs={{0,4},{2,6},{4,0},{6,2},{8,12},{10,14},{12,8},{14,10},{16,20},{18,... | collective-permute-start | bytes 1179656 | tf_op jit(solution)/shard_map/ppermute | solution.py:412
  176.8 12.0 %collective-permute-start.41 = (bf16[48,3072]{1,0:T(8,128)(2,1)S(1)}, bf16[48,3072]{1,0:T(8,128)(2,1)S(1)}, u32[]{:S(2)}, u32[]{:S(2)}) collective-permute-start(bf16[48,3072]{1,0:T(8,128)(2,1)S(1)} %get-tuple-element.231), channel_id=1, source_target_pairs={{0,2},{2,0},{4,6},{6,4},{8,10},{10,8},{12,14},{14,12},{16,18},{18,... | collective-permute-start | bytes 884744 | tf_op jit(solution)/shard_map/ppermute | solution.py:412
  179.1 12.1 %collective-permute-start.43 = (bf16[48,896]{1,0:T(8,128)(2,1)S(1)}, bf16[48,896]{1,0:T(8,128)(2,1)S(1)}, u32[]{:S(2)}, u32[]{:S(2)}) collective-permute-start(bf16[48,896]{1,0:T(8,128)(2,1)S(1)} %get-tuple-element.241), channel_id=1, source_target_pairs={{0,8},{2,10},{4,12},{6,14},{8,16},{10,18},{12,20},{14,22},{16,24},... | collective-permute-start | bytes 258056 | tf_op jit(solution)/shard_map/ppermute | solution.py:416
  179.2 14.8 %collective-permute-start.44 = (bf16[48,896]{1,0:T(8,128)(2,1)S(1)}, bf16[48,896]{1,0:T(8,128)(2,1)S(1)}, u32[]{:S(2)}, u32[]{:S(2)}) collective-permute-start(bf16[48,896]{1,0:T(8,128)(2,1)S(1)} %get-tuple-element.242), channel_id=1, source_target_pairs={{0,16},{2,18},{4,20},{6,22},{8,24},{10,26},{12,28},{14,30},{16,0},... | collective-permute-start | bytes 258056 | tf_op jit(solution)/shard_map/ppermute | solution.py:416
  181.8 12.2 %collective-permute-start.45 = (bf16[48,896]{1,0:T(8,128)(2,1)S(1)}, bf16[48,896]{1,0:T(8,128)(2,1)S(1)}, u32[]{:S(2)}, u32[]{:S(2)}) collective-permute-start(bf16[48,896]{1,0:T(8,128)(2,1)S(1)} %get-tuple-element.243), channel_id=1, source_target_pairs={{0,24},{2,26},{4,28},{6,30},{8,0},{10,2},{12,4},{14,6},{16,8},{18,... | collective-permute-start | bytes 258056 | tf_op jit(solution)/shard_map/ppermute | solution.py:416
  (76 other events, 516.8 us)
where the time goes:
time: 203 us; the launch traced here: 202 us
  Pallas kernels  77.5 us (38%)
  starting transfers between devices  55.1 us (27%)
  waiting for transfers between devices  48.2 us (24%)
  local copies, waits for them, and re-layouts  9.47 us (5%)
  matrix products  8.56 us (4%)
    pallas_call x41, Pallas kernels, whole_call(): pl.pallas_call(kernel, in_specs=[smem] * scalars + [vmem] * (len(inputs)...  75.2 us
    ppermute x21, waiting for transfers between devices, shifted(): lax.ppermute(values, 'dp', [(i, (i + 4 * steps) % count) for i in range(c...  33.5 us
    ppermute x21, starting transfers between devices, shifted(): lax.ppermute(values, 'dp', [(i, (i + 4 * steps) % count) for i in range(c...  28.9 us
    ppermute x21, starting transfers between devices, along(): return lax.ppermute(values, 'dp', pair_up(bit, count))  24.7 us
    ppermute x21, waiting for transfers between devices, along(): return lax.ppermute(values, 'dp', pair_up(bit, count))  13.6 us
    unnamed x100, local copies, waits for them, and re-layouts  9.47 us
    dot_general x4, matrix products, dot_tn(): lax.dot_general(left, right, (((0,), (0,)), ((), ())), preferred_element_...  8.56 us
  transfers between devices with their start and end apart: 50, of which 19 were waited for; matrix products, arithmetic and copies ran while one was open for 4% of the time, Pallas kernels for 34%

commit v1 on v0

--- a/solution.py
+++ b/solution.py
@@ -1239,9 +1239,12 @@
             ffn_right_root[:, 0],
             [ffn_master[:, 0]],
         )
+        sent = late_sum[2](after(second_far[0], ffn_left_new), second_far[1], part=parts[1])
+        second_parts = send_third(*sent, count=count)
+        first_state = slow_state(after(first_state, sent[0]), first_parts[1:])
         wide = high * late_cut
         down_grad, down_left_new, down_right_new, down_new = precondition(
-            [after(down_near, ffn_left_new), *first_far],
+            [after(down_near, first_state), *first_far],
             FBLK,
             down_left,
             down_right,
@@ -1252,10 +1255,7 @@
             starts=[0, wide + 128, wide],
         )
         down_grad, down_new = jnp.swapaxes(down_grad, 2, 3), jnp.swapaxes(down_new, 2, 3)
-        sent = late_sum[2](after(second_far[0], down_left_new), second_far[1], part=parts[1])
-        second_parts = send_third(*sent, count=count)
-        first_state = slow_state(after(first_state, sent[0]), first_parts[1:])
-        first_parts[0] = after(first_parts[0], first_state)
+        first_parts[0] = after(first_parts[0], down_left_new)
         gain_grad, gain_moment_new, gain_new = whole_call(
             gains_kernel,
             [first_state, along(first_state, 2, count), gains, gain_moments],

time: 203 us -> 202 us (level)
  transfers between devices with their start and end apart: 50 -> 50, of which waited for: 19 -> 18; matrix products, arithmetic and copies ran while one was open for 4% -> 4% of each run, Pallas kernels for 34% -> 34%
where the time goes in v1:
time: 202 us
  Pallas kernels  77.5 us (38%)
  starting transfers between devices  55.1 us (27%)
  waiting for transfers between devices  47.6 us (24%)
  local copies, waits for them, and re-layouts  9.47 us (5%)
  matrix products  8.56 us (4%)
    pallas_call x41, Pallas kernels, whole_call(): pl.pallas_call(kernel, in_specs=[smem] * scalars + [vmem] * (len(inputs)...  75.2 us
    ppermute x21, waiting for transfers between devices, shifted(): lax.ppermute(values, 'dp', [(i, (i + 4 * steps) % count) for i in range(c...  33.5 us
    ppermute x21, starting transfers between devices, shifted(): lax.ppermute(values, 'dp', [(i, (i + 4 * steps) % count) for i in range(c...  28.9 us
    ppermute x21, starting transfers between devices, along(): return lax.ppermute(values, 'dp', pair_up(bit, count))  24.7 us
    ppermute x21, waiting for transfers between devices, along(): return lax.ppermute(values, 'dp', pair_up(bit, count))  13 us
    unnamed x100, local copies, waits for them, and re-layouts  9.47 us
    dot_general x4, matrix products, dot_tn(): lax.dot_general(left, right, (((0,), (0,)), ((), ())), preferred_element_...  8.56 us
  transfers between devices with their start and end apart: 50, of which 18 were waited for; matrix products, arithmetic and copies ran while one was open for 4% of the time, Pallas kernels for 34%

profile of v1, /device:TPU:0, one launch (start us, length us, event | category | flops | bytes accessed | tf_op | source)
XLA Modules:
  0.0 201.5 jit_solution(16504253070894861804)
XLA Ops:
  1.3 2.3 %pack.1 = (bf16[48,1536]{1,0:T(8,128)(2,1)}, bf16[48,2048]{1,0:T(8,128)(2,1)}, bf16[48,4608]{1,0:T(8,128)(2,1)}) custom-call(f32[3,8,48,48]{3,2,1,0:T(8,128)} %bitcast.47, f32[1,8,48,48]{3,2,1,0:T(8,128)} %refs_9_.3, f32[2,8,48,128]{3,2,1,0:T(8,128)} %bitcast.58, f32[1,8,48,128]{3,2,1,0:T(8,128)} %bitcast.62), custom_call_target="tpu_custom_call" | custom-call | tf_op jit(solution)/shard_map/pack/pallas_call | solution.py:532
  3.6 3.0 %collective-permute-start.6 = (bf16[48,4608]{1,0:T(8,128)(2,1)}, bf16[48,4608]{1,0:T(8,128)(2,1)}, u32[]{:S(2)}, u32[]{:S(2)}) collective-permute-start(bf16[48,4608]{1,0:T(8,128)(2,1)} %get-tuple-element.172.refs_5_.refs_0_), channel_id=1, source_target_pairs={{0,4},{2,6},{4,0},{6,2},{8,12},{10,14},{12,8},{14,10},{16,20},{18,... | collective-permute-start | bytes 1327112 | tf_op jit(solution)/shard_map/ppermute | solution.py:412
  8.1 3.6 %collective-permute-start.4 = (bf16[48,1536]{1,0:T(8,128)(2,1)}, bf16[48,1536]{1,0:T(8,128)(2,1)S(1)}, u32[]{:S(2)}, u32[]{:S(2)}) collective-permute-start(bf16[48,1536]{1,0:T(8,128)(2,1)} %get-tuple-element.143), channel_id=1, source_target_pairs={{0,24},{2,26},{4,28},{6,30},{8,0},{10,2},{12,4},{14,6},{16,8},{18,... | collective-permute-start | bytes 442376 | tf_op jit(solution)/shard_map/ppermute | solution.py:416
  18.7 3.3 %collective-permute-done.1.refs_0_ = bf16[48,1536]{1,0:T(8,128)(2,1)S(1)} collective-permute-done((bf16[48,1536]{1,0:T(8,128)(2,1)}, bf16[48,1536]{1,0:T(8,128)(2,1)S(1)}, u32[]{:S(2)}, u32[]{:S(2)}) %collective-permute-start.1) | collective-permute-done | bytes 147488 | tf_op jit(solution)/shard_map/ppermute | solution.py:416
  33.1 12.6 %collective-permute-done.10.refs_3_ = bf16[48,2048]{1,0:T(8,128)(2,1)S(1)} collective-permute-done((bf16[48,2048]{1,0:T(8,128)(2,1)S(1)}, bf16[48,2048]{1,0:T(8,128)(2,1)S(1)}, u32[]{:S(2)}, u32[]{:S(2)}) %collective-permute-start.10) | collective-permute-done | bytes 196640 | tf_op jit(solution)/shard_map/ppermute | solution.py:416
  45.8 2.4 %end_round_two.1 = (bf16[48,2304]{1,0:T(8,128)(2,1)}, bf16[48,2304]{1,0:T(8,128)(2,1)}, bf16[48,6144]{1,0:T(8,128)(2,1)S(1)}, bf16[48,4096]{1,0:T(8,128)(2,1)S(1)}) custom-call(bf16[48,6912]{1,0:T(8,128)(2,1)S(1)} %collective-permute-done.7.refs_0_.refs_4_.refs_3_, bf16[48,6912]{1,0:T(8,128)(2,1)S(1)} %collective-permute-done.8.refs_1_.refs_5_.refs_4_, ...), custom_call_target="tpu_custom_call" | custom-call | tf_op jit(solution)/shard_map/end_round_two/pallas_call | solution.py:64
  64.4 2.9 %project.1 = (bf16[1024,768]{1,0:T(8,128)(2,1)S(1)}, bf16[1024,384]{1,0:T(8,128)(2,1)S(1)}, bf16[1024,384]{1,0:T(8,128)(2,1)S(1)}, bf16[1024,384]{1,0:T(8,128)(2,1)S(1)}) custom-call(bf16[1024,768]{1,0:T(8,128)(2,1)S(1)} %in_order.2.x_ref, f32[2,768]{1,0:T(2,128)S(1)} %copy-done.47, bf16[768,1152]{1,0:T(8,128)(2,1)S(1)} %get-tuple-element.158.w_ref, ...), custom_call_target="tpu_custom_call" | custom-call | tf_op jit(solution)/shard_map/project/pallas_call | solution.py:64
  67.3 7.8 %attend.1 = (bf16[1024,384]{1,0:T(8,128)(2,1)S(1)}, f32[24,1024]{1,0:T(8,128)S(1)}) custom-call(bf16[1024,384]{1,0:T(8,128)(2,1)S(1)} %get-tuple-element.159.q_ref, bf16[1024,384]{1,0:T(8,128)(2,1)S(1)} %get-tuple-element.160.k_ref, bf16[1024,384]{1,0:T(8,128)(2,1)S(1)} %get-tuple-element.161.v_ref), custom_call_target="tpu_custom_call" | custom-call | tf_op jit(solution)/shard_map/attend/pallas_call | solution.py:64
  78.2 6.6 %collective-permute-done.21.refs_1_ = bf16[48,3072]{1,0:T(8,128)(2,1)S(1)} collective-permute-done((bf16[48,3072]{1,0:T(8,128)(2,1)S(1)}, bf16[48,3072]{1,0:T(8,128)(2,1)S(1)}, u32[]{:S(2)}, u32[]{:S(2)}) %collective-permute-start.21) | collective-permute-done | bytes 294944 | tf_op jit(solution)/shard_map/ppermute | solution.py:412
  86.7 7.1 %ffn.1 = (f32[1024,768]{1,0:T(8,128)S(1)}, bf16[1024,768]{1,0:T(8,128)(2,1)S(1)}, f32[1024,1024]{1,0:T(8,128)S(1)}, f32[1024,1024]{1,0:T(8,128)S(1)}, bf16[1024,1024]{1,0:T(8,128)(2,1)S(1)}) custom-call(bf16[1024,768]{1,0:T(8,128)(2,1)S(1)} %in_order.2.x_ref, bf16[1024,384]{1,0:T(8,128)(2,1)S(1)} %get-tuple-element.168.o_ref, ...), custom_call_target="tpu_custom_call" | custom-call | tf_op jit(solution)/shard_map/ffn/pallas_call | solution.py:64
  99.1 8.1 %ffn_back.1 = (bf16[1024,2048]{1,0:T(8,128)(2,1)S(1)}, bf16[1024,768]{1,0:T(8,128)(2,1)S(1)}) custom-call(bf16[1024,768]{1,0:T(8,128)(2,1)S(1)} %in_order.3.cot_ref, f32[1024,1024]{1,0:T(8,128)S(1)} %get-tuple-element.181.gate_ref, f32[1024,1024]{1,0:T(8,128)S(1)} %get-tuple-element.182.up_ref, bf16[768,1024]{1,0:T(8,128)(2,1)S(1)} %place_down.1.wdt_ref, ...), custom_call_target="tpu_custom_call" | custom-call | tf_op jit(solution)/shard_map/ffn_back/pallas_call | solution.py:64
  109.9 3.6 %fusion.5.refs_0_ = f32[768,2048]{1,0:T(8,128)S(1)} fusion(bf16[1024,768]{1,0:T(8,128)(2,1)S(1)} %get-tuple-element.189, bf16[1024,2048]{1,0:T(8,128)(2,1)S(1)} %get-tuple-element.191), kind=kOutput, calls=%fused_computation.10 | convolution fusion | flops 3221225472 | bytes 12058624 | tf_op jit(solution)/shard_map/dot_general | solution.py:50
  115.6 2.5 %middle_back.1 = (f32[1024,768]{1,0:T(8,128)S(1)}, bf16[1024,768]{1,0:T(8,128)(2,1)S(1)}, bf16[1024,384]{1,0:T(8,128)(2,1)S(1)}, f32[1,768]{1,0:T(1,128)S(1)}) custom-call(bf16[1024,768]{1,0:T(8,128)(2,1)S(1)} %in_order.3.cot_ref, f32[1024,768]{1,0:T(8,128)S(1)} %get-tuple-element.204.x1_ref, bf16[1024,768]{1,0:T(8,128)(2,1)S(1)} %get-tuple-element.188.near_ref, ...), custom_call_target="tpu_custom_call" | custom-call | tf_op jit(solution)/shard_map/middle_back/pallas_call | solution.py:64
  121.4 3.4 %collective-permute-done.25.refs_1_ = bf16[48,4096]{1,0:T(8,128)(2,1)S(1)} collective-permute-done((bf16[48,4096]{1,0:T(8,128)(2,1)S(1)}, bf16[48,4096]{1,0:T(8,128)(2,1)S(1)}, u32[]{:S(2)}, u32[]{:S(2)}) %collective-permute-start.25) | collective-permute-done | bytes 393248 | tf_op jit(solution)/shard_map/ppermute | solution.py:412
  128.9 14.0 %attend_back.1.dqkv_ref = bf16[1024,1152]{1,0:T(8,128)(2,1)S(1)} custom-call(bf16[1024,384]{1,0:T(8,128)(2,1)S(1)} %get-tuple-element.159.q_ref, bf16[1024,384]{1,0:T(8,128)(2,1)S(1)} %get-tuple-element.160.k_ref, bf16[1024,384]{1,0:T(8,128)(2,1)S(1)} %copy-done.11, bf16[1024,384]{1,0:T(8,128)(2,1)S(1)} %get-tuple-element.202.do_ref, ...), custom_call_target="tpu_custom_call" | custom-call | tf_op jit(solution)/shard_map/attend_back/pallas_call | solution.py:64
  153.2 3.4 %collective-permute-start.34 = (bf16[48,2048]{1,0:T(8,128)(2,1)S(1)}, bf16[48,2048]{1,0:T(8,128)(2,1)S(1)}, u32[]{:S(2)}, u32[]{:S(2)}) collective-permute-start(bf16[48,2048]{1,0:T(8,128)(2,1)S(1)} %get-tuple-element.218), channel_id=1, source_target_pairs={{0,24},{2,26},{4,28},{6,30},{8,0},{10,2},{12,4},{14,6},{16,8},{18,... | collective-permute-start | bytes 589832 | tf_op jit(solution)/shard_map/ppermute | solution.py:416
  156.6 2.5 %input_back.1 = (bf16[1024,768]{1,0:T(8,128)(2,1)S(1)}, f32[1,768]{1,0:T(1,128)S(1)}) custom-call(bf16[1024,768]{1,0:T(8,128)(2,1)S(1)} %in_order.2.x_ref, bf16[1024,1152]{1,0:T(8,128)(2,1)S(1)} %attend_back.1.dqkv_ref, bf16[768,1152]{1,0:T(8,128)(2,1)S(1)} %get-tuple-element.158.w_ref), custom_call_target="tpu_custom_call" | custom-call | tf_op jit(solution)/shard_map/input_back/pallas_call | solution.py:64
  169.3 7.4 %collective-permute-done.40.refs_3_ = bf16[48,2048]{1,0:T(8,128)(2,1)S(1)} collective-permute-done((bf16[48,2048]{1,0:T(8,128)(2,1)S(1)}, bf16[48,2048]{1,0:T(8,128)(2,1)S(1)}, u32[]{:S(2)}, u32[]{:S(2)}) %collective-permute-start.40) | collective-permute-done | bytes 196640 | tf_op jit(solution)/shard_map/ppermute | solution.py:416
  179.2 2.7 %collective-permute-start.44 = (bf16[48,896]{1,0:T(8,128)(2,1)S(1)}, bf16[48,896]{1,0:T(8,128)(2,1)S(1)}, u32[]{:S(2)}, u32[]{:S(2)}) collective-permute-start(bf16[48,896]{1,0:T(8,128)(2,1)S(1)} %get-tuple-element.240), channel_id=1, source_target_pairs={{0,16},{2,18},{4,20},{6,22},{8,24},{10,26},{12,28},{14,30},{16,0},... | collective-permute-start | bytes 258056 | tf_op jit(solution)/shard_map/ppermute | solution.py:416
  183.0 3.1 %precondition.4 = (f32[2,8,48,128]{3,2,1,0:T(8,128)}, f32[2,8,48,48]{3,2,1,0:T(8,128)}, f32[2,8,128,128]{3,2,1,0:T(8,128)}, f32[2,8,48,128]{3,2,1,0:T(8,128)}) custom-call(f32[48,2048]{1,0:T(8,128)S(1)} %get-tuple-element.233.refs_0_, bf16[48,2048]{1,0:T(8,128)(2,1)S(1)} %collective-permute-done.33.refs_1_, ...), custom_call_target="tpu_custom_call" | custom-call | tf_op jit(solution)/shard_map/precondition/pallas_call | solution.py:64
  188.4 2.8 %collective-permute-start.49 = (bf16[48,768]{1,0:T(8,128)(2,1)S(1)}, bf16[48,768]{1,0:T(8,128)(2,1)S(1)}, u32[]{:S(2)}, u32[]{:S(2)}) collective-permute-start(bf16[48,768]{1,0:T(8,128)(2,1)S(1)} %get-tuple-element.252), channel_id=1, source_target_pairs={{0,24},{2,26},{4,28},{6,30},{8,0},{10,2},{12,4},{14,6},{16,8},{18,... | collective-permute-start | bytes 221192 | tf_op jit(solution)/shard_map/ppermute | solution.py:416
  192.0 2.6 %precondition.5 = (f32[1,8,48,128]{3,2,1,0:T(8,128)}, f32[1,8,128,128]{3,2,1,0:T(8,128)}, f32[1,8,48,48]{3,2,1,0:T(8,128)}, f32[1,8,48,128]{3,2,1,0:T(8,128)}) custom-call(f32[48,4096]{1,0:T(8,128)S(1)} %ring_add.5.refs_2_.refs_5_.refs_0_, bf16[48,4224]{1,0:T(8,128)(2,1)S(1)} %collective-permute-done.38.refs_2_.refs_1_, ...), custom_call_target="tpu_custom_call" | custom-call | tf_op jit(solution)/shard_map/precondition/pallas_call | solution.py:64
  194.6 2.4 %precondition.6 = (f32[4,8,48,48]{3,2,1,0:T(8,128)S(1)}, f32[4,8,48,48]{3,2,1,0:T(8,128)S(1)}, f32[4,8,48,48]{3,2,1,0:T(8,128)S(1)}, f32[3,8,48,48]{3,2,1,0:T(8,128)S(1)}, f32[1,8,48,48]{3,2,1,0:T(8,128)S(1)}) custom-call(f32[48,768]{1,0:T(8,128)S(1)} %get-tuple-element.247.refs_0_, bf16[48,896]{1,0:T(8,128)(2,1)S(1)} %collective-permute-done.43.refs_0_.refs_1_, ...), custom_call_target="tpu_custom_call" | custom-call | tf_op jit(solution)/shard_map/precondition/pallas_call | solution.py:64
  197.7 3.8 %precondition.7 = (f32[4,8,48,48]{3,2,1,0:T(8,128)}, f32[4,8,48,48]{3,2,1,0:T(8,128)}, f32[4,8,48,48]{3,2,1,0:T(8,128)}, f32[3,8,48,48]{3,2,1,0:T(8,128)}, f32[1,8,48,48]{3,2,1,0:T(8,128)}) custom-call(f32[48,768]{1,0:T(8,128)S(1)} %get-tuple-element.249.refs_0_, bf16[48,768]{1,0:T(8,128)(2,1)S(1)} %collective-permute-done.47.refs_1_, ...), custom_call_target="tpu_custom_call" | custom-call | tf_op jit(solution)/shard_map/precondition/pallas_call | solution.py:64
  (225 shorter events, 86.0 us)
Async XLA Ops:
  3.6 20.5 %collective-permute-start.6 = (bf16[48,4608]{1,0:T(8,128)(2,1)}, bf16[48,4608]{1,0:T(8,128)(2,1)}, u32[]{:S(2)}, u32[]{:S(2)}) collective-permute-start(bf16[48,4608]{1,0:T(8,128)(2,1)} %get-tuple-element.172.refs_5_.refs_0_), channel_id=1, source_target_pairs={{0,4},{2,6},{4,0},{6,2},{8,12},{10,14},{12,8},{14,10},{16,20},{18,... | collective-permute-start | bytes 1327112 | tf_op jit(solution)/shard_map/ppermute | solution.py:412
  6.6 17.5 %collective-permute-start.5 = (bf16[48,4608]{1,0:T(8,128)(2,1)}, bf16[48,4608]{1,0:T(8,128)(2,1)}, u32[]{:S(2)}, u32[]{:S(2)}) collective-permute-start(bf16[48,4608]{1,0:T(8,128)(2,1)} %get-tuple-element.172.refs_5_.refs_0_), channel_id=1, source_target_pairs={{0,2},{2,0},{4,6},{6,4},{8,10},{10,8},{12,14},{14,12},{16,18},{18,... | collective-permute-start | bytes 1327112 | tf_op jit(solution)/shard_map/ppermute | solution.py:412
  8.1 13.9 %collective-permute-start.4 = (bf16[48,1536]{1,0:T(8,128)(2,1)}, bf16[48,1536]{1,0:T(8,128)(2,1)S(1)}, u32[]{:S(2)}, u32[]{:S(2)}) collective-permute-start(bf16[48,1536]{1,0:T(8,128)(2,1)} %get-tuple-element.143), channel_id=1, source_target_pairs={{0,24},{2,26},{4,28},{6,30},{8,0},{10,2},{12,4},{14,6},{16,8},{18,... | collective-permute-start | bytes 442376 | tf_op jit(solution)/shard_map/ppermute | solution.py:416
  11.7 12.3 %collective-permute-start.3 = (bf16[48,1536]{1,0:T(8,128)(2,1)}, bf16[48,1536]{1,0:T(8,128)(2,1)S(1)}, u32[]{:S(2)}, u32[]{:S(2)}) collective-permute-start(bf16[48,1536]{1,0:T(8,128)(2,1)} %get-tuple-element.143), channel_id=1, source_target_pairs={{0,16},{2,18},{4,20},{6,22},{8,24},{10,26},{12,28},{14,30},{16,0},... | collective-permute-start | bytes 442376 | tf_op jit(solution)/shard_map/ppermute | solution.py:416
  25.3 20.4 %collective-permute-start.8 = (bf16[48,6912]{1,0:T(8,128)(2,1)S(1)}, bf16[48,6912]{1,0:T(8,128)(2,1)S(1)}, u32[]{:S(2)}, u32[]{:S(2)}) collective-permute-start(bf16[48,6912]{1,0:T(8,128)(2,1)S(1)} %get-tuple-element.149), channel_id=1, source_target_pairs={{0,4},{2,6},{4,0},{6,2},{8,12},{10,14},{12,8},{14,10},{16,20},{18,... | collective-permute-start | bytes 1990664 | tf_op jit(solution)/shard_map/ppermute | solution.py:412
  25.9 19.9 %collective-permute-start.7 = (bf16[48,6912]{1,0:T(8,128)(2,1)S(1)}, bf16[48,6912]{1,0:T(8,128)(2,1)S(1)}, u32[]{:S(2)}, u32[]{:S(2)}) collective-permute-start(bf16[48,6912]{1,0:T(8,128)(2,1)S(1)} %get-tuple-element.148.refs_3_), channel_id=1, source_target_pairs={{0,2},{2,0},{4,6},{6,4},{8,10},{10,8},{12,14},{14,12},{16,18},{18,... | collective-permute-start | bytes 1990664 | tf_op jit(solution)/shard_map/ppermute | solution.py:412
  27.8 17.9 %collective-permute-start.10 = (bf16[48,2048]{1,0:T(8,128)(2,1)S(1)}, bf16[48,2048]{1,0:T(8,128)(2,1)S(1)}, u32[]{:S(2)}, u32[]{:S(2)}) collective-permute-start(bf16[48,2048]{1,0:T(8,128)(2,1)S(1)} %copy-done.49), channel_id=1, source_target_pairs={{0,16},{2,18},{4,20},{6,22},{8,24},{10,26},{12,28},{14,30},{16,0},... | collective-permute-start | bytes 589832 | tf_op jit(solution)/shard_map/ppermute | solution.py:416
  29.3 16.5 %collective-permute-start.9 = (bf16[48,2048]{1,0:T(8,128)(2,1)S(1)}, bf16[48,2048]{1,0:T(8,128)(2,1)S(1)}, u32[]{:S(2)}, u32[]{:S(2)}) collective-permute-start(bf16[48,2048]{1,0:T(8,128)(2,1)S(1)} %copy-done.49), channel_id=1, source_target_pairs={{0,8},{2,10},{4,12},{6,14},{8,16},{10,18},{12,20},{14,22},{16,24},... | collective-permute-start | bytes 589832 | tf_op jit(solution)/shard_map/ppermute | solution.py:416
  60.1 15.1 %collective-permute-start.15 = (bf16[48,6144]{1,0:T(8,128)(2,1)S(1)}, bf16[48,6144]{1,0:T(8,128)(2,1)S(1)}, u32[]{:S(2)}, u32[]{:S(2)}) collective-permute-start(bf16[48,6144]{1,0:T(8,128)(2,1)S(1)} %copy-done.38), channel_id=1, source_target_pairs={{0,2},{2,0},{4,6},{6,4},{8,10},{10,8},{12,14},{14,12},{16,18},{18,... | collective-permute-start | bytes 1769480 | tf_op jit(solution)/shard_map/ppermute | solution.py:412
  61.6 13.6 %collective-permute-start.17 = (bf16[48,6144]{1,0:T(8,128)(2,1)S(1)}, bf16[48,6144]{1,0:T(8,128)(2,1)S(1)}, u32[]{:S(2)}, u32[]{:S(2)}) collective-permute-start(bf16[48,6144]{1,0:T(8,128)(2,1)S(1)} %copy-done.38), channel_id=1, source_target_pairs={{0,4},{2,6},{4,0},{6,2},{8,12},{10,14},{12,8},{14,10},{16,20},{18,... | collective-permute-start | bytes 1769480 | tf_op jit(solution)/shard_map/ppermute | solution.py:412
  63.1 12.1 %collective-permute-start.16 = (bf16[48,4096]{1,0:T(8,128)(2,1)}, bf16[48,4096]{1,0:T(8,128)(2,1)S(1)}, u32[]{:S(2)}, u32[]{:S(2)}) collective-permute-start(bf16[48,4096]{1,0:T(8,128)(2,1)} %collective-permute-done.14.refs_1_), channel_id=1, source_target_pairs={{0,8},{2,10},{4,12},{6,14},{8,16},{10,18},{12,20},{14,22},{16,24},... | collective-permute-start | bytes 1179656 | tf_op jit(solution)/shard_map/ppermute | solution.py:416
  75.2 11.5 %collective-permute-start.18 = (bf16[1024,384]{1,0:T(8,128)(2,1)S(1)}, bf16[1024,384]{1,0:T(8,128)(2,1)S(1)}, u32[]{:S(2)}, u32[]{:S(2)}) collective-permute-start(bf16[1024,384]{1,0:T(8,128)(2,1)S(1)} %get-tuple-element.168.o_ref), channel_id=1, source_target_pairs={{0,1},{1,0},{2,3},{3,2},{4,5},{5,4},{6,7},{7,6},{8,9},{9,8},{10,11... | collective-permute-start | bytes 2359304 | tf_op jit(solution)/shard_map/ppermute | solution.py:420
  85.3 12.3 %collective-permute-start.22 = (bf16[48,4096]{1,0:T(8,128)(2,1)S(1)}, bf16[48,4096]{1,0:T(8,128)(2,1)S(1)}, u32[]{:S(2)}, u32[]{:S(2)}) collective-permute-start(bf16[48,4096]{1,0:T(8,128)(2,1)S(1)} %collective-permute-done.16.refs_2_), channel_id=1, source_target_pairs={{0,8},{2,10},{4,12},{6,14},{8,16},{10,18},{12,20},{14,22},{16,24},... | collective-permute-start | bytes 1179656 | tf_op jit(solution)/shard_map/ppermute | solution.py:416
  96.2 11.6 %collective-permute-start.23 = (bf16[48,4096]{1,0:T(8,128)(2,1)S(1)}, bf16[48,4096]{1,0:T(8,128)(2,1)S(1)}, u32[]{:S(2)}, u32[]{:S(2)}) collective-permute-start(bf16[48,4096]{1,0:T(8,128)(2,1)S(1)} %get-tuple-element.179), channel_id=1, source_target_pairs={{0,8},{2,10},{4,12},{6,14},{8,16},{10,18},{12,20},{14,22},{16,24},... | collective-permute-start | bytes 1179656 | tf_op jit(solution)/shard_map/ppermute | solution.py:416
  108.0 13.3 %collective-permute-start.26 = (bf16[48,4096]{1,0:T(8,128)(2,1)S(1)}, bf16[48,4096]{1,0:T(8,128)(2,1)S(1)}, u32[]{:S(2)}, u32[]{:S(2)}) collective-permute-start(bf16[48,4096]{1,0:T(8,128)(2,1)S(1)} %ring_add.3), channel_id=1, source_target_pairs={{0,8},{2,10},{4,12},{6,14},{8,16},{10,18},{12,20},{14,22},{16,24},... | collective-permute-start | bytes 1179656 | tf_op jit(solution)/shard_map/ppermute | solution.py:416
  125.3 17.6 %collective-permute-start.28 = (bf16[1024,768]{1,0:T(8,128)(2,1)S(1)}, bf16[1024,768]{1,0:T(8,128)(2,1)S(1)}, u32[]{:S(2)}, u32[]{:S(2)}) collective-permute-start(bf16[1024,768]{1,0:T(8,128)(2,1)S(1)} %ffn_out.1.near_ref), channel_id=1, source_target_pairs={{0,1},{1,0},{2,3},{3,2},{4,5},{5,4},{6,7},{7,6},{8,9},{9,8},{10,11... | collective-permute-start | bytes 4718600 | tf_op jit(solution)/shard_map/ppermute | solution.py:420
  125.4 20.0 %collective-permute-start.29 = (bf16[48,8192]{1,0:T(8,128)(2,1)S(1)}, bf16[48,8192]{1,0:T(8,128)(2,1)S(1)}, u32[]{:S(2)}, u32[]{:S(2)}) collective-permute-start(bf16[48,8192]{1,0:T(8,128)(2,1)S(1)} %get-tuple-element.201), channel_id=1, source_target_pairs={{0,2},{2,0},{4,6},{6,4},{8,10},{10,8},{12,14},{14,12},{16,18},{18,... | collective-permute-start | bytes 2359304 | tf_op jit(solution)/shard_map/ppermute | solution.py:412
  126.9 19.6 %collective-permute-start.30 = (bf16[48,8192]{1,0:T(8,128)(2,1)S(1)}, bf16[48,8192]{1,0:T(8,128)(2,1)S(1)}, u32[]{:S(2)}, u32[]{:S(2)}) collective-permute-start(bf16[48,8192]{1,0:T(8,128)(2,1)S(1)} %get-tuple-element.208), channel_id=1, source_target_pairs={{0,4},{2,6},{4,0},{6,2},{8,12},{10,14},{12,8},{14,10},{16,20},{18,... | collective-permute-start | bytes 2359304 | tf_op jit(solution)/shard_map/ppermute | solution.py:412
  128.4 15.6 %collective-permute-start.31 = (bf16[48,4096]{1,0:T(8,128)(2,1)S(1)}, bf16[48,4096]{1,0:T(8,128)(2,1)S(1)}, u32[]{:S(2)}, u32[]{:S(2)}) collective-permute-start(bf16[48,4096]{1,0:T(8,128)(2,1)S(1)} %ring_add.4), channel_id=1, source_target_pairs={{0,8},{2,10},{4,12},{6,14},{8,16},{10,18},{12,20},{14,22},{16,24},... | collective-permute-start | bytes 1179656 | tf_op jit(solution)/shard_map/ppermute | solution.py:416
  150.6 12.1 %collective-permute-start.32 = (bf16[48,3584]{1,0:T(8,128)(2,1)S(1)}, bf16[48,3584]{1,0:T(8,128)(2,1)S(1)}, u32[]{:S(2)}, u32[]{:S(2)}) collective-permute-start(bf16[48,3584]{1,0:T(8,128)(2,1)S(1)} %get-tuple-element.214), channel_id=1, source_target_pairs={{0,4},{2,6},{4,0},{6,2},{8,12},{10,14},{12,8},{14,10},{16,20},{18,... | collective-permute-start | bytes 1032200 | tf_op jit(solution)/shard_map/ppermute | solution.py:412
  163.0 13.8 %collective-permute-start.38 = (bf16[48,4224]{1,0:T(8,128)(2,1)S(1)}, bf16[48,4224]{1,0:T(8,128)(2,1)S(1)}, u32[]{:S(2)}, u32[]{:S(2)}) collective-permute-start(bf16[48,4224]{1,0:T(8,128)(2,1)S(1)} %get-tuple-element.223), channel_id=1, source_target_pairs={{0,2},{2,0},{4,6},{6,4},{8,10},{10,8},{12,14},{14,12},{16,18},{18,... | collective-permute-start | bytes 1216520 | tf_op jit(solution)/shard_map/ppermute | solution.py:412
  164.4 12.3 %collective-permute-start.39 = (bf16[48,4096]{1,0:T(8,128)(2,1)S(1)}, bf16[48,4096]{1,0:T(8,128)(2,1)S(1)}, u32[]{:S(2)}, u32[]{:S(2)}) collective-permute-start(bf16[48,4096]{1,0:T(8,128)(2,1)S(1)} %get-tuple-element.225), channel_id=1, source_target_pairs={{0,4},{2,6},{4,0},{6,2},{8,12},{10,14},{12,8},{14,10},{16,20},{18,... | collective-permute-start | bytes 1179656 | tf_op jit(solution)/shard_map/ppermute | solution.py:412
  165.0 11.8 %collective-permute-start.40 = (bf16[48,2048]{1,0:T(8,128)(2,1)S(1)}, bf16[48,2048]{1,0:T(8,128)(2,1)S(1)}, u32[]{:S(2)}, u32[]{:S(2)}) collective-permute-start(bf16[48,2048]{1,0:T(8,128)(2,1)S(1)} %get-tuple-element.230), channel_id=1, source_target_pairs={{0,16},{2,18},{4,20},{6,22},{8,24},{10,26},{12,28},{14,30},{16,0},... | collective-permute-start | bytes 589832 | tf_op jit(solution)/shard_map/ppermute | solution.py:416
  179.2 12.1 %collective-permute-start.44 = (bf16[48,896]{1,0:T(8,128)(2,1)S(1)}, bf16[48,896]{1,0:T(8,128)(2,1)S(1)}, u32[]{:S(2)}, u32[]{:S(2)}) collective-permute-start(bf16[48,896]{1,0:T(8,128)(2,1)S(1)} %get-tuple-element.240), channel_id=1, source_target_pairs={{0,16},{2,18},{4,20},{6,22},{8,24},{10,26},{12,28},{14,30},{16,0},... | collective-permute-start | bytes 258056 | tf_op jit(solution)/shard_map/ppermute | solution.py:416
  (76 other events, 518.6 us)

commit v2 on v1

--- a/solution.py
+++ b/solution.py
@@ -903,12 +903,9 @@
                     at = block * width
                     update(which, here, matrix, block, row[:, at : at + width])
             else:
-
-                @pl.loop(0, HALF_GRID // 4)
-                def _(step):
-                    for block in [4 * step + number for number in range(4)]:
-                        lanes = pl.ds(pl.multiple_of(start + block * width, 128), width)
-                        update(which, here, matrix, block, total_ref[:, lanes])
+                for block in range(HALF_GRID):
+                    lanes = pl.ds(pl.multiple_of(start + block * width, 128), width)
+                    update(which, here, matrix, block, total_ref[:, lanes])
 
         if len({spots[matrix][0] for matrix in matrices}) == 1:
 

time: 202 us -> 202 us (level)
  no operation moved by 1% of the time
where the time goes in v2:
time: 202 us; the launch traced here: 201 us
  Pallas kernels  77.2 us (38%)
  starting transfers between devices  55.1 us (27%)
  waiting for transfers between devices  47.6 us (24%)
  local copies, waits for them, and re-layouts  9.47 us (5%)
  matrix products  8.56 us (4%)
    pallas_call x41, Pallas kernels, whole_call(): pl.pallas_call(kernel, in_specs=[smem] * scalars + [vmem] * (len(inputs)...  74.8 us
    ppermute x21, waiting for transfers between devices, shifted(): lax.ppermute(values, 'dp', [(i, (i + 4 * steps) % count) for i in range(c...  33.5 us
    ppermute x21, starting transfers between devices, shifted(): lax.ppermute(values, 'dp', [(i, (i + 4 * steps) % count) for i in range(c...  28.9 us
    ppermute x21, starting transfers between devices, along(): return lax.ppermute(values, 'dp', pair_up(bit, count))  24.7 us
    ppermute x21, waiting for transfers between devices, along(): return lax.ppermute(values, 'dp', pair_up(bit, count))  13 us
    unnamed x100, local copies, waits for them, and re-layouts  9.47 us
    dot_general x4, matrix products, dot_tn(): lax.dot_general(left, right, (((0,), (0,)), ((), ())), preferred_element_...  8.56 us
  transfers between devices with their start and end apart: 50, of which 18 were waited for; matrix products, arithmetic and copies ran while one was open for 4% of the time, Pallas kernels for 34%

profile of v2, /device:TPU:0, one launch (start us, length us, event | category | flops | bytes accessed | tf_op | source)
XLA Modules:
  0.0 201.2 jit_solution(16291753479845425413)
XLA Ops:
  1.3 2.3 %pack.1 = (bf16[48,1536]{1,0:T(8,128)(2,1)}, bf16[48,2048]{1,0:T(8,128)(2,1)}, bf16[48,4608]{1,0:T(8,128)(2,1)}) custom-call(f32[3,8,48,48]{3,2,1,0:T(8,128)} %bitcast.47, f32[1,8,48,48]{3,2,1,0:T(8,128)} %refs_9_.3, f32[2,8,48,128]{3,2,1,0:T(8,128)} %bitcast.58, f32[1,8,48,128]{3,2,1,0:T(8,128)} %bitcast.62), custom_call_target="tpu_custom_call" | custom-call | tf_op jit(solution)/shard_map/pack/pallas_call | solution.py:532
  3.6 3.0 %collective-permute-start.6 = (bf16[48,4608]{1,0:T(8,128)(2,1)}, bf16[48,4608]{1,0:T(8,128)(2,1)}, u32[]{:S(2)}, u32[]{:S(2)}) collective-permute-start(bf16[48,4608]{1,0:T(8,128)(2,1)} %get-tuple-element.172.refs_5_.refs_0_), channel_id=1, source_target_pairs={{0,4},{2,6},{4,0},{6,2},{8,12},{10,14},{12,8},{14,10},{16,20},{18,... | collective-permute-start | bytes 1327112 | tf_op jit(solution)/shard_map/ppermute | solution.py:412
  8.1 3.6 %collective-permute-start.4 = (bf16[48,1536]{1,0:T(8,128)(2,1)}, bf16[48,1536]{1,0:T(8,128)(2,1)S(1)}, u32[]{:S(2)}, u32[]{:S(2)}) collective-permute-start(bf16[48,1536]{1,0:T(8,128)(2,1)} %get-tuple-element.143), channel_id=1, source_target_pairs={{0,24},{2,26},{4,28},{6,30},{8,0},{10,2},{12,4},{14,6},{16,8},{18,... | collective-permute-start | bytes 442376 | tf_op jit(solution)/shard_map/ppermute | solution.py:416
  18.7 3.3 %collective-permute-done.1.refs_0_ = bf16[48,1536]{1,0:T(8,128)(2,1)S(1)} collective-permute-done((bf16[48,1536]{1,0:T(8,128)(2,1)}, bf16[48,1536]{1,0:T(8,128)(2,1)S(1)}, u32[]{:S(2)}, u32[]{:S(2)}) %collective-permute-start.1) | collective-permute-done | bytes 147488 | tf_op jit(solution)/shard_map/ppermute | solution.py:416
  33.1 12.6 %collective-permute-done.10.refs_3_ = bf16[48,2048]{1,0:T(8,128)(2,1)S(1)} collective-permute-done((bf16[48,2048]{1,0:T(8,128)(2,1)S(1)}, bf16[48,2048]{1,0:T(8,128)(2,1)S(1)}, u32[]{:S(2)}, u32[]{:S(2)}) %collective-permute-start.10) | collective-permute-done | bytes 196640 | tf_op jit(solution)/shard_map/ppermute | solution.py:416
  45.8 2.4 %end_round_two.1 = (bf16[48,2304]{1,0:T(8,128)(2,1)}, bf16[48,2304]{1,0:T(8,128)(2,1)}, bf16[48,6144]{1,0:T(8,128)(2,1)S(1)}, bf16[48,4096]{1,0:T(8,128)(2,1)S(1)}) custom-call(bf16[48,6912]{1,0:T(8,128)(2,1)S(1)} %collective-permute-done.7.refs_0_.refs_4_.refs_3_, bf16[48,6912]{1,0:T(8,128)(2,1)S(1)} %collective-permute-done.8.refs_1_.refs_5_.refs_4_, ...), custom_call_target="tpu_custom_call" | custom-call | tf_op jit(solution)/shard_map/end_round_two/pallas_call | solution.py:64
  64.4 2.9 %project.1 = (bf16[1024,768]{1,0:T(8,128)(2,1)S(1)}, bf16[1024,384]{1,0:T(8,128)(2,1)S(1)}, bf16[1024,384]{1,0:T(8,128)(2,1)S(1)}, bf16[1024,384]{1,0:T(8,128)(2,1)S(1)}) custom-call(bf16[1024,768]{1,0:T(8,128)(2,1)S(1)} %in_order.2.x_ref, f32[2,768]{1,0:T(2,128)S(1)} %copy-done.47, bf16[768,1152]{1,0:T(8,128)(2,1)S(1)} %get-tuple-element.158.w_ref, ...), custom_call_target="tpu_custom_call" | custom-call | tf_op jit(solution)/shard_map/project/pallas_call | solution.py:64
  67.3 7.8 %attend.1 = (bf16[1024,384]{1,0:T(8,128)(2,1)S(1)}, f32[24,1024]{1,0:T(8,128)S(1)}) custom-call(bf16[1024,384]{1,0:T(8,128)(2,1)S(1)} %get-tuple-element.159.q_ref, bf16[1024,384]{1,0:T(8,128)(2,1)S(1)} %get-tuple-element.160.k_ref, bf16[1024,384]{1,0:T(8,128)(2,1)S(1)} %get-tuple-element.161.v_ref), custom_call_target="tpu_custom_call" | custom-call | tf_op jit(solution)/shard_map/attend/pallas_call | solution.py:64
  78.2 6.6 %collective-permute-done.21.refs_1_ = bf16[48,3072]{1,0:T(8,128)(2,1)S(1)} collective-permute-done((bf16[48,3072]{1,0:T(8,128)(2,1)S(1)}, bf16[48,3072]{1,0:T(8,128)(2,1)S(1)}, u32[]{:S(2)}, u32[]{:S(2)}) %collective-permute-start.21) | collective-permute-done | bytes 294944 | tf_op jit(solution)/shard_map/ppermute | solution.py:412
  86.7 7.1 %ffn.1 = (f32[1024,768]{1,0:T(8,128)S(1)}, bf16[1024,768]{1,0:T(8,128)(2,1)S(1)}, f32[1024,1024]{1,0:T(8,128)S(1)}, f32[1024,1024]{1,0:T(8,128)S(1)}, bf16[1024,1024]{1,0:T(8,128)(2,1)S(1)}) custom-call(bf16[1024,768]{1,0:T(8,128)(2,1)S(1)} %in_order.2.x_ref, bf16[1024,384]{1,0:T(8,128)(2,1)S(1)} %get-tuple-element.168.o_ref, ...), custom_call_target="tpu_custom_call" | custom-call | tf_op jit(solution)/shard_map/ffn/pallas_call | solution.py:64
  99.1 8.1 %ffn_back.1 = (bf16[1024,2048]{1,0:T(8,128)(2,1)S(1)}, bf16[1024,768]{1,0:T(8,128)(2,1)S(1)}) custom-call(bf16[1024,768]{1,0:T(8,128)(2,1)S(1)} %in_order.3.cot_ref, f32[1024,1024]{1,0:T(8,128)S(1)} %get-tuple-element.181.gate_ref, f32[1024,1024]{1,0:T(8,128)S(1)} %get-tuple-element.182.up_ref, bf16[768,1024]{1,0:T(8,128)(2,1)S(1)} %place_down.1.wdt_ref, ...), custom_call_target="tpu_custom_call" | custom-call | tf_op jit(solution)/shard_map/ffn_back/pallas_call | solution.py:64
  109.9 3.6 %fusion.5.refs_0_ = f32[768,2048]{1,0:T(8,128)S(1)} fusion(bf16[1024,768]{1,0:T(8,128)(2,1)S(1)} %get-tuple-element.189, bf16[1024,2048]{1,0:T(8,128)(2,1)S(1)} %get-tuple-element.191), kind=kOutput, calls=%fused_computation.10 | convolution fusion | flops 3221225472 | bytes 12058624 | tf_op jit(solution)/shard_map/dot_general | solution.py:50
  115.6 2.5 %middle_back.1 = (f32[1024,768]{1,0:T(8,128)S(1)}, bf16[1024,768]{1,0:T(8,128)(2,1)S(1)}, bf16[1024,384]{1,0:T(8,128)(2,1)S(1)}, f32[1,768]{1,0:T(1,128)S(1)}) custom-call(bf16[1024,768]{1,0:T(8,128)(2,1)S(1)} %in_order.3.cot_ref, f32[1024,768]{1,0:T(8,128)S(1)} %get-tuple-element.204.x1_ref, bf16[1024,768]{1,0:T(8,128)(2,1)S(1)} %get-tuple-element.188.near_ref, ...), custom_call_target="tpu_custom_call" | custom-call | tf_op jit(solution)/shard_map/middle_back/pallas_call | solution.py:64
  121.4 3.4 %collective-permute-done.25.refs_1_ = bf16[48,4096]{1,0:T(8,128)(2,1)S(1)} collective-permute-done((bf16[48,4096]{1,0:T(8,128)(2,1)S(1)}, bf16[48,4096]{1,0:T(8,128)(2,1)S(1)}, u32[]{:S(2)}, u32[]{:S(2)}) %collective-permute-start.25) | collective-permute-done | bytes 393248 | tf_op jit(solution)/shard_map/ppermute | solution.py:412
  128.9 14.0 %attend_back.1.dqkv_ref = bf16[1024,1152]{1,0:T(8,128)(2,1)S(1)} custom-call(bf16[1024,384]{1,0:T(8,128)(2,1)S(1)} %get-tuple-element.159.q_ref, bf16[1024,384]{1,0:T(8,128)(2,1)S(1)} %get-tuple-element.160.k_ref, bf16[1024,384]{1,0:T(8,128)(2,1)S(1)} %copy-done.11, bf16[1024,384]{1,0:T(8,128)(2,1)S(1)} %get-tuple-element.202.do_ref, ...), custom_call_target="tpu_custom_call" | custom-call | tf_op jit(solution)/shard_map/attend_back/pallas_call | solution.py:64
  153.2 3.4 %collective-permute-start.34 = (bf16[48,2048]{1,0:T(8,128)(2,1)S(1)}, bf16[48,2048]{1,0:T(8,128)(2,1)S(1)}, u32[]{:S(2)}, u32[]{:S(2)}) collective-permute-start(bf16[48,2048]{1,0:T(8,128)(2,1)S(1)} %get-tuple-element.218), channel_id=1, source_target_pairs={{0,24},{2,26},{4,28},{6,30},{8,0},{10,2},{12,4},{14,6},{16,8},{18,... | collective-permute-start | bytes 589832 | tf_op jit(solution)/shard_map/ppermute | solution.py:416
  156.6 2.5 %input_back.1 = (bf16[1024,768]{1,0:T(8,128)(2,1)S(1)}, f32[1,768]{1,0:T(1,128)S(1)}) custom-call(bf16[1024,768]{1,0:T(8,128)(2,1)S(1)} %in_order.2.x_ref, bf16[1024,1152]{1,0:T(8,128)(2,1)S(1)} %attend_back.1.dqkv_ref, bf16[768,1152]{1,0:T(8,128)(2,1)S(1)} %get-tuple-element.158.w_ref), custom_call_target="tpu_custom_call" | custom-call | tf_op jit(solution)/shard_map/input_back/pallas_call | solution.py:64
  169.3 7.4 %collective-permute-done.40.refs_3_ = bf16[48,2048]{1,0:T(8,128)(2,1)S(1)} collective-permute-done((bf16[48,2048]{1,0:T(8,128)(2,1)S(1)}, bf16[48,2048]{1,0:T(8,128)(2,1)S(1)}, u32[]{:S(2)}, u32[]{:S(2)}) %collective-permute-start.40) | collective-permute-done | bytes 196640 | tf_op jit(solution)/shard_map/ppermute | solution.py:416
  179.2 2.7 %collective-permute-start.44 = (bf16[48,896]{1,0:T(8,128)(2,1)S(1)}, bf16[48,896]{1,0:T(8,128)(2,1)S(1)}, u32[]{:S(2)}, u32[]{:S(2)}) collective-permute-start(bf16[48,896]{1,0:T(8,128)(2,1)S(1)} %get-tuple-element.240), channel_id=1, source_target_pairs={{0,16},{2,18},{4,20},{6,22},{8,24},{10,26},{12,28},{14,30},{16,0},... | collective-permute-start | bytes 258056 | tf_op jit(solution)/shard_map/ppermute | solution.py:416
  183.0 3.0 %precondition.4 = (f32[2,8,48,128]{3,2,1,0:T(8,128)}, f32[2,8,48,48]{3,2,1,0:T(8,128)}, f32[2,8,128,128]{3,2,1,0:T(8,128)}, f32[2,8,48,128]{3,2,1,0:T(8,128)}) custom-call(f32[48,2048]{1,0:T(8,128)S(1)} %get-tuple-element.233.refs_0_, bf16[48,2048]{1,0:T(8,128)(2,1)S(1)} %collective-permute-done.33.refs_1_, ...), custom_call_target="tpu_custom_call" | custom-call | tf_op jit(solution)/shard_map/precondition/pallas_call | solution.py:64
  188.4 2.8 %collective-permute-start.49 = (bf16[48,768]{1,0:T(8,128)(2,1)S(1)}, bf16[48,768]{1,0:T(8,128)(2,1)S(1)}, u32[]{:S(2)}, u32[]{:S(2)}) collective-permute-start(bf16[48,768]{1,0:T(8,128)(2,1)S(1)} %get-tuple-element.252), channel_id=1, source_target_pairs={{0,24},{2,26},{4,28},{6,30},{8,0},{10,2},{12,4},{14,6},{16,8},{18,... | collective-permute-start | bytes 221192 | tf_op jit(solution)/shard_map/ppermute | solution.py:416
  191.9 2.4 %precondition.5 = (f32[1,8,48,128]{3,2,1,0:T(8,128)}, f32[1,8,128,128]{3,2,1,0:T(8,128)}, f32[1,8,48,48]{3,2,1,0:T(8,128)}, f32[1,8,48,128]{3,2,1,0:T(8,128)}) custom-call(f32[48,4096]{1,0:T(8,128)S(1)} %ring_add.5.refs_2_.refs_5_.refs_0_, bf16[48,4224]{1,0:T(8,128)(2,1)S(1)} %collective-permute-done.38.refs_2_.refs_1_, ...), custom_call_target="tpu_custom_call" | custom-call | tf_op jit(solution)/shard_map/precondition/pallas_call | solution.py:64
  194.3 2.4 %precondition.6 = (f32[4,8,48,48]{3,2,1,0:T(8,128)S(1)}, f32[4,8,48,48]{3,2,1,0:T(8,128)S(1)}, f32[4,8,48,48]{3,2,1,0:T(8,128)S(1)}, f32[3,8,48,48]{3,2,1,0:T(8,128)S(1)}, f32[1,8,48,48]{3,2,1,0:T(8,128)S(1)}) custom-call(f32[48,768]{1,0:T(8,128)S(1)} %get-tuple-element.247.refs_0_, bf16[48,896]{1,0:T(8,128)(2,1)S(1)} %collective-permute-done.43.refs_0_.refs_1_, ...), custom_call_target="tpu_custom_call" | custom-call | tf_op jit(solution)/shard_map/precondition/pallas_call | solution.py:64
  197.4 3.8 %precondition.7 = (f32[4,8,48,48]{3,2,1,0:T(8,128)}, f32[4,8,48,48]{3,2,1,0:T(8,128)}, f32[4,8,48,48]{3,2,1,0:T(8,128)}, f32[3,8,48,48]{3,2,1,0:T(8,128)}, f32[1,8,48,48]{3,2,1,0:T(8,128)}) custom-call(f32[48,768]{1,0:T(8,128)S(1)} %get-tuple-element.249.refs_0_, bf16[48,768]{1,0:T(8,128)(2,1)S(1)} %collective-permute-done.47.refs_1_, ...), custom_call_target="tpu_custom_call" | custom-call | tf_op jit(solution)/shard_map/precondition/pallas_call | solution.py:64
  (225 shorter events, 86.0 us)
Async XLA Ops:
  3.6 20.5 %collective-permute-start.6 = (bf16[48,4608]{1,0:T(8,128)(2,1)}, bf16[48,4608]{1,0:T(8,128)(2,1)}, u32[]{:S(2)}, u32[]{:S(2)}) collective-permute-start(bf16[48,4608]{1,0:T(8,128)(2,1)} %get-tuple-element.172.refs_5_.refs_0_), channel_id=1, source_target_pairs={{0,4},{2,6},{4,0},{6,2},{8,12},{10,14},{12,8},{14,10},{16,20},{18,... | collective-permute-start | bytes 1327112 | tf_op jit(solution)/shard_map/ppermute | solution.py:412
  6.6 17.5 %collective-permute-start.5 = (bf16[48,4608]{1,0:T(8,128)(2,1)}, bf16[48,4608]{1,0:T(8,128)(2,1)}, u32[]{:S(2)}, u32[]{:S(2)}) collective-permute-start(bf16[48,4608]{1,0:T(8,128)(2,1)} %get-tuple-element.172.refs_5_.refs_0_), channel_id=1, source_target_pairs={{0,2},{2,0},{4,6},{6,4},{8,10},{10,8},{12,14},{14,12},{16,18},{18,... | collective-permute-start | bytes 1327112 | tf_op jit(solution)/shard_map/ppermute | solution.py:412
  8.1 13.9 %collective-permute-start.4 = (bf16[48,1536]{1,0:T(8,128)(2,1)}, bf16[48,1536]{1,0:T(8,128)(2,1)S(1)}, u32[]{:S(2)}, u32[]{:S(2)}) collective-permute-start(bf16[48,1536]{1,0:T(8,128)(2,1)} %get-tuple-element.143), channel_id=1, source_target_pairs={{0,24},{2,26},{4,28},{6,30},{8,0},{10,2},{12,4},{14,6},{16,8},{18,... | collective-permute-start | bytes 442376 | tf_op jit(solution)/shard_map/ppermute | solution.py:416
  11.7 12.3 %collective-permute-start.3 = (bf16[48,1536]{1,0:T(8,128)(2,1)}, bf16[48,1536]{1,0:T(8,128)(2,1)S(1)}, u32[]{:S(2)}, u32[]{:S(2)}) collective-permute-start(bf16[48,1536]{1,0:T(8,128)(2,1)} %get-tuple-element.143), channel_id=1, source_target_pairs={{0,16},{2,18},{4,20},{6,22},{8,24},{10,26},{12,28},{14,30},{16,0},... | collective-permute-start | bytes 442376 | tf_op jit(solution)/shard_map/ppermute | solution.py:416
  25.3 20.4 %collective-permute-start.8 = (bf16[48,6912]{1,0:T(8,128)(2,1)S(1)}, bf16[48,6912]{1,0:T(8,128)(2,1)S(1)}, u32[]{:S(2)}, u32[]{:S(2)}) collective-permute-start(bf16[48,6912]{1,0:T(8,128)(2,1)S(1)} %get-tuple-element.149), channel_id=1, source_target_pairs={{0,4},{2,6},{4,0},{6,2},{8,12},{10,14},{12,8},{14,10},{16,20},{18,... | collective-permute-start | bytes 1990664 | tf_op jit(solution)/shard_map/ppermute | solution.py:412
  25.9 19.9 %collective-permute-start.7 = (bf16[48,6912]{1,0:T(8,128)(2,1)S(1)}, bf16[48,6912]{1,0:T(8,128)(2,1)S(1)}, u32[]{:S(2)}, u32[]{:S(2)}) collective-permute-start(bf16[48,6912]{1,0:T(8,128)(2,1)S(1)} %get-tuple-element.148.refs_3_), channel_id=1, source_target_pairs={{0,2},{2,0},{4,6},{6,4},{8,10},{10,8},{12,14},{14,12},{16,18},{18,... | collective-permute-start | bytes 1990664 | tf_op jit(solution)/shard_map/ppermute | solution.py:412
  27.8 17.9 %collective-permute-start.10 = (bf16[48,2048]{1,0:T(8,128)(2,1)S(1)}, bf16[48,2048]{1,0:T(8,128)(2,1)S(1)}, u32[]{:S(2)}, u32[]{:S(2)}) collective-permute-start(bf16[48,2048]{1,0:T(8,128)(2,1)S(1)} %copy-done.49), channel_id=1, source_target_pairs={{0,16},{2,18},{4,20},{6,22},{8,24},{10,26},{12,28},{14,30},{16,0},... | collective-permute-start | bytes 589832 | tf_op jit(solution)/shard_map/ppermute | solution.py:416
  29.3 16.5 %collective-permute-start.9 = (bf16[48,2048]{1,0:T(8,128)(2,1)S(1)}, bf16[48,2048]{1,0:T(8,128)(2,1)S(1)}, u32[]{:S(2)}, u32[]{:S(2)}) collective-permute-start(bf16[48,2048]{1,0:T(8,128)(2,1)S(1)} %copy-done.49), channel_id=1, source_target_pairs={{0,8},{2,10},{4,12},{6,14},{8,16},{10,18},{12,20},{14,22},{16,24},... | collective-permute-start | bytes 589832 | tf_op jit(solution)/shard_map/ppermute | solution.py:416
  60.1 15.1 %collective-permute-start.15 = (bf16[48,6144]{1,0:T(8,128)(2,1)S(1)}, bf16[48,6144]{1,0:T(8,128)(2,1)S(1)}, u32[]{:S(2)}, u32[]{:S(2)}) collective-permute-start(bf16[48,6144]{1,0:T(8,128)(2,1)S(1)} %copy-done.38), channel_id=1, source_target_pairs={{0,2},{2,0},{4,6},{6,4},{8,10},{10,8},{12,14},{14,12},{16,18},{18,... | collective-permute-start | bytes 1769480 | tf_op jit(solution)/shard_map/ppermute | solution.py:412
  61.6 13.6 %collective-permute-start.17 = (bf16[48,6144]{1,0:T(8,128)(2,1)S(1)}, bf16[48,6144]{1,0:T(8,128)(2,1)S(1)}, u32[]{:S(2)}, u32[]{:S(2)}) collective-permute-start(bf16[48,6144]{1,0:T(8,128)(2,1)S(1)} %copy-done.38), channel_id=1, source_target_pairs={{0,4},{2,6},{4,0},{6,2},{8,12},{10,14},{12,8},{14,10},{16,20},{18,... | collective-permute-start | bytes 1769480 | tf_op jit(solution)/shard_map/ppermute | solution.py:412
  63.1 12.1 %collective-permute-start.16 = (bf16[48,4096]{1,0:T(8,128)(2,1)}, bf16[48,4096]{1,0:T(8,128)(2,1)S(1)}, u32[]{:S(2)}, u32[]{:S(2)}) collective-permute-start(bf16[48,4096]{1,0:T(8,128)(2,1)} %collective-permute-done.14.refs_1_), channel_id=1, source_target_pairs={{0,8},{2,10},{4,12},{6,14},{8,16},{10,18},{12,20},{14,22},{16,24},... | collective-permute-start | bytes 1179656 | tf_op jit(solution)/shard_map/ppermute | solution.py:416
  75.2 11.5 %collective-permute-start.18 = (bf16[1024,384]{1,0:T(8,128)(2,1)S(1)}, bf16[1024,384]{1,0:T(8,128)(2,1)S(1)}, u32[]{:S(2)}, u32[]{:S(2)}) collective-permute-start(bf16[1024,384]{1,0:T(8,128)(2,1)S(1)} %get-tuple-element.168.o_ref), channel_id=1, source_target_pairs={{0,1},{1,0},{2,3},{3,2},{4,5},{5,4},{6,7},{7,6},{8,9},{9,8},{10,11... | collective-permute-start | bytes 2359304 | tf_op jit(solution)/shard_map/ppermute | solution.py:420
  85.3 12.3 %collective-permute-start.22 = (bf16[48,4096]{1,0:T(8,128)(2,1)S(1)}, bf16[48,4096]{1,0:T(8,128)(2,1)S(1)}, u32[]{:S(2)}, u32[]{:S(2)}) collective-permute-start(bf16[48,4096]{1,0:T(8,128)(2,1)S(1)} %collective-permute-done.16.refs_2_), channel_id=1, source_target_pairs={{0,8},{2,10},{4,12},{6,14},{8,16},{10,18},{12,20},{14,22},{16,24},... | collective-permute-start | bytes 1179656 | tf_op jit(solution)/shard_map/ppermute | solution.py:416
  96.2 11.6 %collective-permute-start.23 = (bf16[48,4096]{1,0:T(8,128)(2,1)S(1)}, bf16[48,4096]{1,0:T(8,128)(2,1)S(1)}, u32[]{:S(2)}, u32[]{:S(2)}) collective-permute-start(bf16[48,4096]{1,0:T(8,128)(2,1)S(1)} %get-tuple-element.179), channel_id=1, source_target_pairs={{0,8},{2,10},{4,12},{6,14},{8,16},{10,18},{12,20},{14,22},{16,24},... | collective-permute-start | bytes 1179656 | tf_op jit(solution)/shard_map/ppermute | solution.py:416
  108.0 13.3 %collective-permute-start.26 = (bf16[48,4096]{1,0:T(8,128)(2,1)S(1)}, bf16[48,4096]{1,0:T(8,128)(2,1)S(1)}, u32[]{:S(2)}, u32[]{:S(2)}) collective-permute-start(bf16[48,4096]{1,0:T(8,128)(2,1)S(1)} %ring_add.3), channel_id=1, source_target_pairs={{0,8},{2,10},{4,12},{6,14},{8,16},{10,18},{12,20},{14,22},{16,24},... | collective-permute-start | bytes 1179656 | tf_op jit(solution)/shard_map/ppermute | solution.py:416
  125.3 17.6 %collective-permute-start.28 = (bf16[1024,768]{1,0:T(8,128)(2,1)S(1)}, bf16[1024,768]{1,0:T(8,128)(2,1)S(1)}, u32[]{:S(2)}, u32[]{:S(2)}) collective-permute-start(bf16[1024,768]{1,0:T(8,128)(2,1)S(1)} %ffn_out.1.near_ref), channel_id=1, source_target_pairs={{0,1},{1,0},{2,3},{3,2},{4,5},{5,4},{6,7},{7,6},{8,9},{9,8},{10,11... | collective-permute-start | bytes 4718600 | tf_op jit(solution)/shard_map/ppermute | solution.py:420
  125.4 20.0 %collective-permute-start.29 = (bf16[48,8192]{1,0:T(8,128)(2,1)S(1)}, bf16[48,8192]{1,0:T(8,128)(2,1)S(1)}, u32[]{:S(2)}, u32[]{:S(2)}) collective-permute-start(bf16[48,8192]{1,0:T(8,128)(2,1)S(1)} %get-tuple-element.201), channel_id=1, source_target_pairs={{0,2},{2,0},{4,6},{6,4},{8,10},{10,8},{12,14},{14,12},{16,18},{18,... | collective-permute-start | bytes 2359304 | tf_op jit(solution)/shard_map/ppermute | solution.py:412
  126.9 19.6 %collective-permute-start.30 = (bf16[48,8192]{1,0:T(8,128)(2,1)S(1)}, bf16[48,8192]{1,0:T(8,128)(2,1)S(1)}, u32[]{:S(2)}, u32[]{:S(2)}) collective-permute-start(bf16[48,8192]{1,0:T(8,128)(2,1)S(1)} %get-tuple-element.208), channel_id=1, source_target_pairs={{0,4},{2,6},{4,0},{6,2},{8,12},{10,14},{12,8},{14,10},{16,20},{18,... | collective-permute-start | bytes 2359304 | tf_op jit(solution)/shard_map/ppermute | solution.py:412
  128.4 15.6 %collective-permute-start.31 = (bf16[48,4096]{1,0:T(8,128)(2,1)S(1)}, bf16[48,4096]{1,0:T(8,128)(2,1)S(1)}, u32[]{:S(2)}, u32[]{:S(2)}) collective-permute-start(bf16[48,4096]{1,0:T(8,128)(2,1)S(1)} %ring_add.4), channel_id=1, source_target_pairs={{0,8},{2,10},{4,12},{6,14},{8,16},{10,18},{12,20},{14,22},{16,24},... | collective-permute-start | bytes 1179656 | tf_op jit(solution)/shard_map/ppermute | solution.py:416
  150.6 12.1 %collective-permute-start.32 = (bf16[48,3584]{1,0:T(8,128)(2,1)S(1)}, bf16[48,3584]{1,0:T(8,128)(2,1)S(1)}, u32[]{:S(2)}, u32[]{:S(2)}) collective-permute-start(bf16[48,3584]{1,0:T(8,128)(2,1)S(1)} %get-tuple-element.214), channel_id=1, source_target_pairs={{0,4},{2,6},{4,0},{6,2},{8,12},{10,14},{12,8},{14,10},{16,20},{18,... | collective-permute-start | bytes 1032200 | tf_op jit(solution)/shard_map/ppermute | solution.py:412
  163.0 13.8 %collective-permute-start.38 = (bf16[48,4224]{1,0:T(8,128)(2,1)S(1)}, bf16[48,4224]{1,0:T(8,128)(2,1)S(1)}, u32[]{:S(2)}, u32[]{:S(2)}) collective-permute-start(bf16[48,4224]{1,0:T(8,128)(2,1)S(1)} %get-tuple-element.223), channel_id=1, source_target_pairs={{0,2},{2,0},{4,6},{6,4},{8,10},{10,8},{12,14},{14,12},{16,18},{18,... | collective-permute-start | bytes 1216520 | tf_op jit(solution)/shard_map/ppermute | solution.py:412
  164.4 12.3 %collective-permute-start.39 = (bf16[48,4096]{1,0:T(8,128)(2,1)S(1)}, bf16[48,4096]{1,0:T(8,128)(2,1)S(1)}, u32[]{:S(2)}, u32[]{:S(2)}) collective-permute-start(bf16[48,4096]{1,0:T(8,128)(2,1)S(1)} %get-tuple-element.225), channel_id=1, source_target_pairs={{0,4},{2,6},{4,0},{6,2},{8,12},{10,14},{12,8},{14,10},{16,20},{18,... | collective-permute-start | bytes 1179656 | tf_op jit(solution)/shard_map/ppermute | solution.py:412
  165.0 11.8 %collective-permute-start.40 = (bf16[48,2048]{1,0:T(8,128)(2,1)S(1)}, bf16[48,2048]{1,0:T(8,128)(2,1)S(1)}, u32[]{:S(2)}, u32[]{:S(2)}) collective-permute-start(bf16[48,2048]{1,0:T(8,128)(2,1)S(1)} %get-tuple-element.230), channel_id=1, source_target_pairs={{0,16},{2,18},{4,20},{6,22},{8,24},{10,26},{12,28},{14,30},{16,0},... | collective-permute-start | bytes 589832 | tf_op jit(solution)/shard_map/ppermute | solution.py:416
  179.2 12.1 %collective-permute-start.44 = (bf16[48,896]{1,0:T(8,128)(2,1)S(1)}, bf16[48,896]{1,0:T(8,128)(2,1)S(1)}, u32[]{:S(2)}, u32[]{:S(2)}) collective-permute-start(bf16[48,896]{1,0:T(8,128)(2,1)S(1)} %get-tuple-element.240), channel_id=1, source_target_pairs={{0,16},{2,18},{4,20},{6,22},{8,24},{10,26},{12,28},{14,30},{16,0},... | collective-permute-start | bytes 258056 | tf_op jit(solution)/shard_map/ppermute | solution.py:416
  (76 other events, 515.8 us)
